TPU v7x, 32 devices: a whole 2x2x4 slice. The times are simulated.
32 devices in a mesh: space: 8 (over y, x, core), mode: 4 (over z).
Axes of the slice: x: 2, y: 2, z: 4, core: 2. Of those that a mesh axis runs over, the one named last changes fastest.
Arguments:
- start_field: float32 [36, 16, 64, 128], P('mode', 'space'), may hold values from -1.8 to 1.8
- source: float32 [36, 16, 64, 128], P('mode', 'space')
- mean_field: float32 [16, 64, 128], P('space'), may hold values from 0.5 to 2
- kl_fields: float32 [4, 16, 64, 128], P(None, 'space'), may hold values from -1 to 1
- triples: int32 [156, 3], replicated, may hold values from 0 to 35, as said below
- coef: float32 [156], replicated, may hold values from 0.5 to 2
Outputs:
- smoothed: float32 [36, 16, 64, 128], P('mode', 'space')
- residual: float32 [36, 16, 64, 128], P('mode', 'space')
Inputs may be any that keep to these rules, and one draw needn't show every extreme that they name: Rows of triples are distinct. Field 0 appears only in the rows (0, s, s), one for every slot s of the 36 slots; the other rows name a field 1 to 4 and two different slots.
All inputs are finite; a program needn't handle non-finite values.
Results may differ from a plain program's by a relative error of at most 0.00022.
Values sent between devices are 32-bit elements; how exact they have to be, the bound alone decides.
A program may use at most 64 MiB of HBM per device.

v0:
```python
import jax
import jax.numpy as jnp
from jax import lax
from jax.sharding import PartitionSpec as P


def extended(block, sides, width):
    for axis, dim in sides:
        count = lax.axis_size(axis)
        forward = [(i, i + 1) for i in range(count - 1)]
        backward = [(target, source) for source, target in forward]
        low = lax.ppermute(
            lax.slice_in_dim(block, block.shape[dim] - width, None, axis=dim), axis, forward
        )
        high = lax.ppermute(lax.slice_in_dim(block, 0, width, axis=dim), axis, backward)
        block = jnp.concatenate([low, block, high], axis=dim)
    return block


def neighbour_views(arr):
    return [
        arr[..., 2:, 1:-1, 1:-1],
        arr[..., :-2, 1:-1, 1:-1],
        arr[..., 1:-1, 2:, 1:-1],
        arr[..., 1:-1, :-2, 1:-1],
        arr[..., 1:-1, 1:-1, 2:],
        arr[..., 1:-1, 1:-1, :-2],
    ]


def stencil(field_pad, coeff_pad):
    centre = field_pad[..., 1:-1, 1:-1, 1:-1]
    own = coeff_pad[..., 1:-1, 1:-1, 1:-1]
    result = None
    for value, other in zip(neighbour_views(field_pad), neighbour_views(coeff_pad)):
        term = 0.5 * (own + other) * (centre - value)
        result = term if result is None else result + term
    return result


def face_total(coeff_pad):
    own = coeff_pad[..., 1:-1, 1:-1, 1:-1]
    result = None
    for other in neighbour_views(coeff_pad):
        term = 0.5 * (own + other)
        result = term if result is None else result + term
    return result


def pad_sides(arr):
    return jnp.pad(arr, [(0, 0)] * (arr.ndim - 2) + [(1, 1), (1, 1)])


def body(start_field, source, mean_field, kl_fields, triples, coef):
    highest = lax.Precision.HIGHEST
    local = start_field.shape[0]
    groups = lax.axis_size("mode")
    slots = local * groups
    nfields = kl_fields.shape[0] + 1
    first_slot = lax.axis_index("mode") * local
    field_ids = (triples[:, 0:1] == jnp.arange(nfields, dtype=jnp.int32)[None]).astype(
        jnp.float32
    ) * coef[:, None]
    row_ids = (triples[:, 1:2] == jnp.arange(slots, dtype=jnp.int32)[None]).astype(jnp.float32)
    col_ids = (triples[:, 2:3] == jnp.arange(slots, dtype=jnp.int32)[None]).astype(jnp.float32)
    coupling = jnp.einsum("nm,ni,nj->mij", field_ids, row_ids, col_ids, precision=highest)
    fields = jnp.concatenate([mean_field[None], kl_fields], axis=0)
    fields_z = extended(fields, (("space", 1),), 1)
    coeff_pad = pad_sides(fields_z)
    mean_faces = face_total(coeff_pad[0])
    mode_diag = jnp.diagonal(coupling[0])
    rows_here = lax.dynamic_slice_in_dim(coupling, first_slot, local, axis=1)
    scaling = (
        lax.dynamic_slice_in_dim(mode_diag, first_slot, local)[:, None, None, None]
        * mean_faces[None]
    )

    def operator(field):
        field_z = extended(field, (("space", 1),), 1)
        mixed = jnp.einsum(
            "mij,jzxy->mizxy",
            rows_here,
            lax.all_gather(field_z, "mode", axis=0, tiled=True),
            precision=highest,
        )
        return jnp.sum(stencil(pad_sides(mixed), coeff_pad[:, None]), axis=0)

    first = source - operator(start_field)
    middle = start_field + 0.8 * first / scaling
    residual = source - operator(middle)
    smoothed = middle + 0.8 * residual / scaling
    return (smoothed, residual)


def solution(mesh):
    return jax.shard_map(
        body,
        mesh=mesh,
        in_specs=(
            P("mode", "space", None, None),
            P("mode", "space", None, None),
            P("space", None, None),
            P(None, "space", None, None),
            P(),
            P(),
        ),
        out_specs=(P("mode", "space", None, None), P("mode", "space", None, None)),
        check_vma=False,
    )
```

profile of v0, /device:TPU:0, one launch (start us, length us, event | category | flops | bytes accessed | tf_op | source)
XLA Modules:
  0.0 291.9 jit_solution(17910114968510789259)
XLA Ops:
  7.3 1.1 fusion.79
  8.4 2.4 collective-permute-start.2
  10.8 1.3 collective-permute-start.3
  12.1 4.3 %collective-permute-done.3 = f32[9,1,64,128]{3,2,1,0:T(8,128)S(1)} collective-permute-done((f32[9,1,64,128]{3,2,1,0:T(8,128)S(1)}, f32[9,1,64,128]{3,2,1,0:T(8,128)S(1)}, u32[]{:S(2)}, u32[]{:S(2)}) %collective-permute-start.3) | collective-permute-done | bytes 294944 | tf_op jit(solution)/shard_map/ppermute | solution.py:15
  16.4 2.2 pad_maximum_fusion.1
  18.7 1.0 fusion.58
  19.7 7.4 %collective-permute-start = (f32[5,1,64,128]{3,2,1,0:T(8,128)S(1)}, f32[5,1,64,128]{3,2,1,0:T(8,128)S(1)}, u32[]{:S(2)}, u32[]{:S(2)}) collective-permute-start(f32[5,1,64,128]{3,2,1,0:T(8,128)S(1)} %get-tuple-element.20), channel_id=1, source_target_pairs={{0,4},{4,8},{8,12},{12,16},{16,20},{20,24},{24,28},{1,5},{5,9},{9,... | collective-permute-start | bytes 491528 | tf_op jit(solution)/shard_map/ppermute | solution.py:12
  27.1 1.3 collective-permute-start.1
  28.7 1.0 gather_fusion
  29.8 0.6 collective-permute-done.1
  32.1 82.0 %all-gather.3.cloned.1.call-done = f32[36,4,64,128]{3,2,1,0:T(8,128)} async-done(((f32[9,4,64,128]{3,2,1,0:T(8,128)}), f32[36,4,64,128]{3,2,1,0:T(8,128)}) %all-gather.3.cloned.1.call-update) | async-done | bytes 4718608 | tf_op jit(solution)/shard_map/all_gather | solution.py:83
  114.1 15.9 %fusion.32 = f32[5,9,4,64,128]{4,1,3,2,0:T(8,128)} fusion(f32[36,4,64,128]{3,2,1,0:T(8,128)} %all-gather.3.cloned.1.call-done, f32[36,5,36]{2,0,1:T(8,128)S(1)} %fusion.56, s32[]{:T(128)S(6)} %select_n.8), kind=kOutput, calls=%fused_computation.45 | convolution fusion | flops 637009920 | bytes 10657796 | tf_op jit(solution)/shard_map/mij,jzxy->mizxy/dot_general | solution.py:80
  130.0 14.7 %fusion.37 = f32[9,2,64,128]{3,0,2,1:T(8,128)S(1)} fusion(f32[5,9,4,64,128]{4,1,3,2,0:T(8,128)} %fusion.32, f32[5,2,64,128]{3,2,1,0:T(8,128)S(1)} %get-tuple-element.15, f32[5,2,64,128]{3,2,1,0:T(8,128)S(1)} %get-tuple-element.11, f32[5,2,64,128]{3,2,1,0:T(8,128)S(1)} %get-tuple-element.12, f32[5,2,64,128]{3,2,1,0:T(8,128)S(1)} %get-tuple-element.13, ...), kind=kLoop, calls=%fused_computation.50 | loop fusion | flops 13123584 | bytes 28770304 | tf_op jit(solution)/shard_map/reduce_sum | solution.py:86
  144.7 0.8 fusion.42
  145.6 1.9 collective-permute-start.4
  147.5 1.3 collective-permute-start.5
  149.0 3.5 %collective-permute-done.5 = f32[9,1,64,128]{3,0,2,1:T(8,128)S(1)} collective-permute-done((f32[9,1,64,128]{3,0,2,1:T(8,128)S(1)}, f32[9,1,64,128]{3,0,2,1:T(8,128)S(1)}, u32[]{:S(2)}, u32[]{:S(2)}) %collective-permute-start.5) | collective-permute-done | bytes 294944 | tf_op jit(solution)/shard_map/ppermute | solution.py:15
  152.6 1.4 copy.29
  154.0 96.8 %all-gather.5.cloned.1.call-done = f32[36,4,64,128]{3,2,1,0:T(8,128)} async-done(((f32[9,4,64,128]{3,2,1,0:T(8,128)}), f32[36,4,64,128]{3,2,1,0:T(8,128)}) %all-gather.5.cloned.1.call-update) | async-done | bytes 4718608 | tf_op jit(solution)/shard_map/all_gather | solution.py:83
  250.8 15.9 %fusion.30 = f32[5,9,4,64,128]{4,1,3,2,0:T(8,128)} fusion(f32[36,4,64,128]{3,2,1,0:T(8,128)} %all-gather.5.cloned.1.call-done, f32[36,5,36]{2,0,1:T(8,128)S(1)} %fusion.56, s32[]{:T(128)S(6)} %select_n.8), kind=kOutput, calls=%fused_computation.43 | convolution fusion | flops 637009920 | bytes 10657796 | tf_op jit(solution)/shard_map/mij,jzxy->mizxy/dot_general | solution.py:80
  266.7 14.7 %fusion.36 = f32[9,2,64,128]{3,0,2,1:T(8,128)S(1)} fusion(f32[5,9,4,64,128]{4,1,3,2,0:T(8,128)} %fusion.30, f32[5,2,64,128]{3,2,1,0:T(8,128)S(1)} %get-tuple-element.15, f32[5,2,64,128]{3,2,1,0:T(8,128)S(1)} %get-tuple-element.11, f32[5,2,64,128]{3,2,1,0:T(8,128)S(1)} %get-tuple-element.12, f32[5,2,64,128]{3,2,1,0:T(8,128)S(1)} %get-tuple-element.13, ...), kind=kLoop, calls=%fused_computation.49 | loop fusion | flops 13123584 | bytes 28770304 | tf_op jit(solution)/shard_map/reduce_sum | solution.py:86
  281.4 1.6 fusion.43
  283.1 1.0 copy.32
  284.1 1.0 copy.33
  (33 shorter events, 2.5 us)
Async XLA Ops:
  7.2 23.2 %copy-start.2 = (f32[4,2,64,128]{3,2,1,0:T(8,128)S(1)}, f32[4,2,64,128]{3,2,1,0:T(8,128)}, u32[]{:S(2)}) copy-start(f32[4,2,64,128]{3,2,1,0:T(8,128)} %param.9) | copy-start | bytes 786436
  7.2 23.2 %copy-start.3 = (f32[2,64,128]{2,1,0:T(8,128)S(1)}, f32[2,64,128]{2,1,0:T(8,128)}, u32[]{:S(2)}) copy-start(f32[2,64,128]{2,1,0:T(8,128)} %param.8) | copy-start | bytes 196612
  7.2 21.2 %copy-start.4 = (s32[156,3]{0,1:T(4,128)S(1)}, s32[156,3]{0,1:T(4,128)}, u32[]{:S(2)}) copy-start(s32[156,3]{0,1:T(4,128)} %param.10) | copy-start | bytes 5620
  7.2 21.2 %copy-start.5 = (f32[156]{0:T(256)S(1)}, f32[156]{0:T(256)}, u32[]{:S(2)}) copy-start(f32[156]{0:T(256)} %param.11) | copy-start | bytes 1876
  7.2 106.9 %all-gather.3.cloned.1.call-start = ((), (), s32[]{:S(2)}) async-start(), calls=%async_computation | async-start | bytes 5898240 | tf_op jit(solution)/shard_map/all_gather | solution.py:83
  8.4 3.7 %collective-permute-start.2 = (f32[9,1,64,128]{3,2,1,0:T(8,128)S(1)}, f32[9,1,64,128]{3,2,1,0:T(8,128)S(1)}, u32[]{:S(2)}, u32[]{:S(2)}) collective-permute-start(f32[9,1,64,128]{3,2,1,0:T(8,128)S(1)} %get-tuple-element.18), channel_id=1, source_target_pairs={{0,4},{4,8},{8,12},{12,16},{16,20},{20,24},{24,28},{1,5},{5,9},{9,... | collective-permute-start | bytes 884744 | tf_op jit(solution)/shard_map/ppermute | solution.py:12
  10.8 5.6 %collective-permute-start.3 = (f32[9,1,64,128]{3,2,1,0:T(8,128)S(1)}, f32[9,1,64,128]{3,2,1,0:T(8,128)S(1)}, u32[]{:S(2)}, u32[]{:S(2)}) collective-permute-start(f32[9,1,64,128]{3,2,1,0:T(8,128)S(1)} %get-tuple-element.19), channel_id=1, source_target_pairs={{4,0},{8,4},{12,8},{16,12},{20,16},{24,20},{28,24},{5,1},{9,5},{13... | collective-permute-start | bytes 884744 | tf_op jit(solution)/shard_map/ppermute | solution.py:15
  18.6 232.2 %all-gather.5.cloned.1.call-start = ((), (), s32[]{:S(2)}) async-start(), calls=%async_computation.1 | async-start | bytes 5898240 | tf_op jit(solution)/shard_map/all_gather | solution.py:83
  19.7 10.1 %collective-permute-start = (f32[5,1,64,128]{3,2,1,0:T(8,128)S(1)}, f32[5,1,64,128]{3,2,1,0:T(8,128)S(1)}, u32[]{:S(2)}, u32[]{:S(2)}) collective-permute-start(f32[5,1,64,128]{3,2,1,0:T(8,128)S(1)} %get-tuple-element.20), channel_id=1, source_target_pairs={{0,4},{4,8},{8,12},{12,16},{16,20},{20,24},{24,28},{1,5},{5,9},{9,... | collective-permute-start | bytes 491528 | tf_op jit(solution)/shard_map/ppermute | solution.py:12
  27.1 3.3 %collective-permute-start.1 = (f32[5,1,64,128]{3,2,1,0:T(8,128)S(1)}, f32[5,1,64,128]{3,2,1,0:T(8,128)S(1)}, u32[]{:S(2)}, u32[]{:S(2)}) collective-permute-start(f32[5,1,64,128]{3,2,1,0:T(8,128)S(1)} %get-tuple-element.21), channel_id=1, source_target_pairs={{4,0},{8,4},{12,8},{16,12},{20,16},{24,20},{28,24},{5,1},{9,5},{13... | collective-permute-start | bytes 491528 | tf_op jit(solution)/shard_map/ppermute | solution.py:15
  130.0 14.7 %copy-start = (f32[9,2,64,128]{3,2,1,0:T(8,128)S(1)}, f32[9,2,64,128]{3,2,1,0:T(8,128)}, u32[]{:S(2)}) copy-start(f32[9,2,64,128]{3,2,1,0:T(8,128)} %param.6) | copy-start | bytes 1769476
  130.0 14.8 %copy-start.1 = (f32[9,2,64,128]{3,2,1,0:T(8,128)S(1)}, f32[9,2,64,128]{3,2,1,0:T(8,128)}, u32[]{:S(2)}) copy-start(f32[9,2,64,128]{3,2,1,0:T(8,128)} %param.7) | copy-start | bytes 1769476
  145.6 3.4 %collective-permute-start.4 = (f32[9,1,64,128]{3,0,2,1:T(8,128)S(1)}, f32[9,1,64,128]{3,0,2,1:T(8,128)S(1)}, u32[]{:S(2)}, u32[]{:S(2)}) collective-permute-start(f32[9,1,64,128]{3,0,2,1:T(8,128)S(1)} %get-tuple-element.16), channel_id=1, source_target_pairs={{0,4},{4,8},{8,12},{12,16},{16,20},{20,24},{24,28},{1,5},{5,9},{9,... | collective-permute-start | bytes 884744 | tf_op jit(solution)/shard_map/ppermute | solution.py:12
  147.5 5.0 %collective-permute-start.5 = (f32[9,1,64,128]{3,0,2,1:T(8,128)S(1)}, f32[9,1,64,128]{3,0,2,1:T(8,128)S(1)}, u32[]{:S(2)}, u32[]{:S(2)}) collective-permute-start(f32[9,1,64,128]{3,0,2,1:T(8,128)S(1)} %get-tuple-element.17), channel_id=1, source_target_pairs={{4,0},{8,4},{12,8},{16,12},{20,16},{24,20},{28,24},{5,1},{9,5},{13... | collective-permute-start | bytes 884744 | tf_op jit(solution)/shard_map/ppermute | solution.py:15
Sparse Core Ops, SparseCore 0:
  18.7 95.3 all-gather.2
  154.1 96.6 all-gather.4
where the time goes:
time: 292 us
  waiting for transfers between devices  187 us (64%)
  other arithmetic  37 us (13%)
  matrix products  32 us (11%)
  starting transfers between devices  15.6 us (5%)
  between operations  14.3 us (5%)
  local copies, waits for them, and re-layouts  5.71 us (2%)
    all_gather x2, waiting for transfers between devices, operator(): lax.all_gather(field_z, 'mode', axis=0, tiled=True)  179 us
    dot_general x2, matrix products, operator(): jnp.einsum('mij,jzxy->mizxy', rows_here, lax.all_gather(field_z, 'mode',...  31.8 us
    reduce_sum x2, other arithmetic, operator(): return jnp.sum(stencil(pad_sides(mixed), coeff_pad[:, None]), axis=0)  29.5 us
    ppermute x3, starting transfers between devices, extended(): lax.ppermute(lax.slice_in_dim(block, block.shape[dim] - width, None, axis...  11.6 us
    ppermute x3, waiting for transfers between devices, extended(): lax.ppermute(lax.slice_in_dim(block, 0, width, axis=dim), axis, backward)  8.37 us
  transfers between devices with their start and end apart: 8, of which 6 were waited for; matrix products, arithmetic and copies ran while one was open for 1% of the time, Pallas kernels for 0%

commit v1 on v0

v1 whole, which is shorter than its diff:
```python
import functools

import jax
import jax.numpy as jnp
from jax import lax
from jax.experimental import pallas as pl
from jax.experimental.pallas import tpu as pltpu
from jax.sharding import PartitionSpec as P

MESH = pl.DeviceIdType.MESH
FACES = 6


def round_up(value, multiple):
    return -(-value // multiple) * multiple


def kernel(
    groups, count, table, start, source, mean, kl,
    a_first, a_second, total_out, diag_out,
    coefs, weights, in_first, in_second, out_first, out_second, vt, cmat,
    trade_send, trade_recv, own_sem, plane_send, plane_recv, row_send, row_recv,
):
    local, planes, height, lanes = start.shape
    slots = local * groups
    rows = height // groups
    nfields = kl.shape[0] + 1
    padded = vt.shape[3]
    entries = weights.shape[0] // (planes * height)
    stride = planes * rows
    me = lax.axis_index("mode")
    at = lax.axis_index("space")
    has_left = at > 0
    has_right = at < count - 1

    barrier = pltpu.get_barrier_semaphore()
    for d in range(1, groups):
        pl.semaphore_signal(
            barrier, inc=1, device_id={"mode": lax.rem(me + d, groups)}, device_id_type=MESH
        )

    @pl.when(has_left)
    def _():
        pl.semaphore_signal(barrier, inc=1, device_id={"space": at - 1}, device_id_type=MESH)

    @pl.when(has_right)
    def _():
        pl.semaphore_signal(barrier, inc=1, device_id={"space": at + 1}, device_id_type=MESH)

    for z in range(planes):
        coefs[z + 1, 0] = mean[z]
        for m in range(1, nfields):
            coefs[z + 1, m] = kl[m - 1, z]

    @pl.when(jnp.logical_not(has_left))
    def _():
        coefs[0] = jnp.zeros(coefs.shape[1:], jnp.float32)
        for k in range(2):
            vt[k, 0] = jnp.zeros(vt.shape[2:], jnp.float32)

    @pl.when(jnp.logical_not(has_right))
    def _():
        coefs[planes + 1] = jnp.zeros(coefs.shape[1:], jnp.float32)
        for k in range(2):
            vt[k, planes + 1] = jnp.zeros(vt.shape[2:], jnp.float32)

    @pl.when(me == 0)
    def _():
        for k in range(2):
            for z in range(planes):
                vt[k, z + 1, 0] = jnp.zeros(vt.shape[3:], jnp.float32)

    @pl.when(me == groups - 1)
    def _():
        for k in range(2):
            for z in range(planes):
                vt[k, z + 1, rows + 1] = jnp.zeros(vt.shape[3:], jnp.float32)

    def band(ref, which):
        return ref.at[:, :, pl.ds(pl.multiple_of(which * rows, rows), rows), :]

    def modes(ref, which):
        size = local * stride
        return ref.at[pl.ds(pl.multiple_of(which * size, size), size), :].reshape(
            local, planes, rows, lanes
        )

    def remote(phase, d):
        peer = lax.rem(me + d, groups)
        if phase < 2:
            src = band((start, source)[phase], peer)
            dst = modes((in_first, in_second)[phase], me)
        else:
            src = modes((out_first, out_second)[phase - 2], peer)
            dst = band((a_first, a_second)[phase - 2], me)
        return pltpu.make_async_remote_copy(
            src_ref=src, dst_ref=dst,
            send_sem=trade_send.at[phase, d - 1], recv_sem=trade_recv.at[phase, d - 1],
            device_id={"mode": peer}, device_id_type=MESH,
        )

    def own(phase):
        if phase < 2:
            src = band((start, source)[phase], me)
            dst = modes((in_first, in_second)[phase], me)
        else:
            src = modes((out_first, out_second)[phase - 2], me)
            dst = band((a_first, a_second)[phase - 2], me)
        return pltpu.make_async_copy(src, dst, own_sem.at[phase])

    def trade_start(phase):
        for d in (2, 1, 3) if groups == 4 else range(1, groups):
            remote(phase, d).start()
        own(phase).start()

    def trade_wait_send(phase):
        for d in range(1, groups):
            remote(phase, d).wait_send()

    def trade_wait_recv(phase):
        for d in range(1, groups):
            remote(phase, d).wait_recv()
        own(phase).wait()

    def plane_copy(k, side):
        if k == 2:
            buf, inner = coefs, lambda z: coefs.at[z]
        else:
            buf, inner = vt, lambda z: vt.at[k, z, pl.ds(1, rows)]
        src, dst = (1, planes + 1) if side == 0 else (planes, 0)
        return pltpu.make_async_remote_copy(
            src_ref=inner(src), dst_ref=inner(dst),
            send_sem=plane_send.at[k, side], recv_sem=plane_recv.at[k, side],
            device_id={"space": at - 1 if side == 0 else at + 1}, device_id_type=MESH,
        )

    def plane_start(k, side):
        @pl.when(has_left if side == 0 else has_right)
        def _():
            plane_copy(k, side).start()

    def plane_wait(k):
        for side, sends, gets in ((0, has_left, has_right), (1, has_right, has_left)):
            @pl.when(sends)
            def _():
                plane_copy(k, side).wait_send()

            @pl.when(gets)
            def _():
                plane_copy(k, side).wait_recv()

    has_up = me > 0
    has_down = me < groups - 1

    def row_copy(k, side):
        src, dst = (1, rows + 1) if side == 0 else (rows, 0)
        return pltpu.make_async_remote_copy(
            src_ref=vt.at[k, pl.ds(1, planes), src], dst_ref=vt.at[k, pl.ds(1, planes), dst],
            send_sem=row_send.at[k, side], recv_sem=row_recv.at[k, side],
            device_id={"mode": me - 1 if side == 0 else me + 1}, device_id_type=MESH,
        )

    def row_start(k):
        for side, sends in ((0, has_up), (1, has_down)):
            @pl.when(sends)
            def _():
                row_copy(k, side).start()

    def row_wait(k):
        for side, sends, gets in ((0, has_up, has_down), (1, has_down, has_up)):
            @pl.when(sends)
            def _():
                row_copy(k, side).wait_send()

            @pl.when(gets)
            def _():
                row_copy(k, side).wait_recv()

    pl.semaphore_wait(
        barrier, groups - 1 + has_left.astype(jnp.int32) + has_right.astype(jnp.int32)
    )
    trade_start(0)
    plane_start(2, 0)
    plane_start(2, 1)

    nnz = table.shape[1]
    width = cmat.shape[1]
    fields_row, rows_row, cols_row, coef_row = (table[i:i + 1, :] for i in range(4))
    row_hot = lax.broadcasted_iota(jnp.int32, (padded, nnz), 0).astype(jnp.float32) == rows_row
    key = fields_row * padded + cols_row
    key_hot = lax.broadcasted_iota(jnp.int32, (width, nnz), 0).astype(jnp.float32) == key
    coef_high = coef_row.astype(jnp.bfloat16).astype(jnp.float32)
    row_one = jnp.where(row_hot, 1.0, 0.0).astype(jnp.bfloat16)
    for piece, value in enumerate((coef_high, coef_row - coef_high)):
        spread = jnp.where(key_hot, value, 0.0).astype(jnp.bfloat16)
        part = lax.dot_general(
            row_one, spread, (((1,), (1,)), ((), ())), preferred_element_type=jnp.float32
        )
        cmat[piece * padded:(piece + 1) * padded, :] = part.astype(jnp.bfloat16)
    diag = jnp.sum(
        jnp.where(jnp.logical_and(row_hot, fields_row == 0.0), coef_row, 0.0), axis=1, keepdims=True
    )
    real = lax.broadcasted_iota(jnp.int32, (padded, 1), 0) < slots
    diag = jnp.where(real, diag, 1.0)
    diag_out[...] = jnp.broadcast_to(diag, diag_out.shape)
    step = 0.8 / diag

    plane_wait(2)
    lane = lax.broadcasted_iota(jnp.int32, (height, lanes), 1)
    row = lax.broadcasted_iota(jnp.int32, (height, lanes), 0)
    for z in range(planes):
        for m in range(nfields):
            c = coefs[z + 1, m]
            faces = []
            for axis, size, ids in ((1, lanes, lane), (0, height, row)):
                for shift, edge in ((size - 1, size - 1), (1, 0)):
                    other = jnp.where(ids == edge, 0.0, pltpu.roll(c, shift, axis))
                    faces.append(0.5 * (c + other))
            faces.append(0.5 * (c + coefs[z + 2, m]))
            faces.append(0.5 * (c + coefs[z, m]))
            total = functools.reduce(lambda a, b: a + b, faces)
            faces[0] = jnp.where(lane == lanes - 1, 0.0, faces[0])
            faces[1] = jnp.where(lane == 0, 0.0, faces[1])
            first = z * height * entries
            for f, value in enumerate(faces + [total]):
                weights[pl.ds(first + f * nfields + m, height, stride=entries), :] = value
            if m == 0:
                total_out[z] = total
                weights[pl.ds(first + (FACES + 1) * nfields, height, stride=entries), :] = 1.0 / total

    trade_wait_send(0)
    trade_start(1)
    trade_wait_recv(0)

    fill = jnp.zeros((padded - slots, lanes), jnp.float32)
    half = rows // 2

    def fetch(ref, z, y):
        return ref[pl.ds(z * rows + y, slots, stride=stride), :]

    def spread_weights(z, y):
        base = pl.multiple_of((z * height + me * rows + y) * entries, 8)
        return weights[pl.ds(base, entries), :]

    for z in range(planes):
        def relay(y, carry):
            vt[0, z + 1, y + 1] = jnp.concatenate([fetch(in_first, z, y), fill], axis=0)
            return carry
        lax.fori_loop(0, rows, relay, 0)
        if z == 0:
            plane_start(0, 0)
        if z == planes - 1:
            plane_start(0, 1)
    row_start(0)

    def applied(k, z, y):
        w = spread_weights(z, y)
        centre = vt[k, z + 1, y + 1]
        others = (
            pltpu.roll(centre, lanes - 1, 1), pltpu.roll(centre, 1, 1),
            vt[k, z + 1, y + 2], vt[k, z + 1, y],
            vt[k, z + 2, y + 1], vt[k, z, y + 1],
        )
        parts = []
        for m in range(nfields):
            at_total = FACES * nfields + m
            value = w[at_total:at_total + 1] * centre
            for f in range(FACES):
                at_face = f * nfields + m
                value = value - w[at_face:at_face + 1] * others[f]
            parts.append(value)
        if width > nfields * padded:
            parts.append(jnp.zeros((width - nfields * padded, lanes), jnp.float32))
        return jnp.concatenate(parts, axis=0)

    def sweep(k, out):
        def pair(t, carry):
            z = t // half
            y = 2 * lax.rem(t, half)
            x = jnp.concatenate([applied(k, z, y), applied(k, z, y + 1)], axis=1)
            high = x.astype(jnp.bfloat16)
            low = (x - high.astype(jnp.float32)).astype(jnp.bfloat16)
            both = jnp.dot(cmat[...], high, preferred_element_type=jnp.float32)
            rest = jnp.dot(cmat[:padded, :], low, preferred_element_type=jnp.float32)
            value = both[:padded] + (both[padded:] + rest)
            for i in range(2):
                out[pl.ds(z * rows + y + i, slots, stride=stride), :] = value[
                    :slots, i * lanes:(i + 1) * lanes
                ]
            return carry
        lax.fori_loop(0, planes * half, pair, 0)

    plane_wait(0)
    row_wait(0)
    sweep(0, out_first)
    trade_wait_recv(1)
    trade_wait_send(1)

    for z in range(planes):
        def update(y, carry):
            inverse = spread_weights(z, y)[(FACES + 1) * nfields:(FACES + 1) * nfields + 1]
            first = fetch(in_second, z, y) - fetch(out_first, z, y)
            first = jnp.concatenate([first, fill], axis=0)
            vt[1, z + 1, y + 1] = vt[0, z + 1, y + 1] + first * (step * inverse)
            return carry
        lax.fori_loop(0, rows, update, 0)
        if z == 0:
            plane_start(1, 0)
        if z == planes - 1:
            plane_start(1, 1)
    row_start(1)
    trade_start(2)
    plane_wait(1)
    row_wait(1)
    sweep(1, out_second)
    trade_start(3)
    for phase in (2, 3):
        trade_wait_send(phase)
        trade_wait_recv(phase)


def body(count, start_field, source, mean_field, kl_fields, triples, coef):
    local, planes, height, lanes = start_field.shape
    groups = lax.axis_size("mode")
    slots = local * groups
    nfields = kl_fields.shape[0] + 1
    rows = height // groups
    padded = round_up(slots, 8)
    width = round_up(nfields * padded, 16)
    entries = round_up((FACES + 1) * nfields + 1, 8)
    table = jnp.concatenate([triples.T.astype(jnp.float32), coef[None]], axis=0)
    f32 = jnp.float32
    whole = jax.ShapeDtypeStruct(start_field.shape, f32)
    in_vmem = pl.BlockSpec(memory_space=pltpu.VMEM)
    anywhere = pl.BlockSpec(memory_space=pl.ANY)
    dma = pltpu.SemaphoreType.DMA
    a_first, a_second, totals, diag = pl.pallas_call(
        functools.partial(kernel, groups, count),
        out_shape=(
            whole, whole,
            jax.ShapeDtypeStruct((planes, height, lanes), f32),
            jax.ShapeDtypeStruct((padded, lanes), f32),
        ),
        in_specs=[in_vmem, anywhere, anywhere, in_vmem, in_vmem],
        out_specs=(anywhere, anywhere, in_vmem, in_vmem),
        scratch_shapes=[
            pltpu.VMEM((planes + 2, nfields, height, lanes), f32),
            pltpu.VMEM((planes * height * entries, lanes), f32),
            pltpu.VMEM((slots * planes * rows, lanes), f32),
            pltpu.VMEM((slots * planes * rows, lanes), f32),
            pltpu.VMEM((slots * planes * rows, lanes), f32),
            pltpu.VMEM((slots * planes * rows, lanes), f32),
            pltpu.VMEM((2, planes + 2, rows + 2, padded, lanes), f32),
            pltpu.VMEM((2 * padded, width), jnp.bfloat16),
            dma((4, groups - 1)), dma((4, groups - 1)), dma((4,)),
            dma((3, 2)), dma((3, 2)), dma((2, 2)), dma((2, 2)),
        ],
        compiler_params=pltpu.CompilerParams(
            collective_id=0, has_side_effects=True, vmem_limit_bytes=40 * 1024 * 1024
        ),
        name="sweeps",
    )(table, start_field, source, mean_field, kl_fields)
    first_slot = lax.axis_index("mode") * local
    own_diag = lax.dynamic_slice_in_dim(diag, first_slot, local)[:, 0]
    scaling = own_diag[:, None, None, None] * totals[None]
    middle = start_field + 0.8 * (source - a_first) / scaling
    residual = source - a_second
    return middle + 0.8 * residual / scaling, residual


def solution(mesh):
    return jax.shard_map(
        functools.partial(body, mesh.shape["space"]),
        mesh=mesh,
        in_specs=(
            P("mode", "space", None, None),
            P("mode", "space", None, None),
            P("space", None, None),
            P(None, "space", None, None),
            P(),
            P(),
        ),
        out_specs=(P("mode", "space", None, None), P("mode", "space", None, None)),
        check_vma=False,
    )
```

time: 292 us -> 73.7 us (0.25)
  waiting for transfers between devices: 187 us -> 0 us
  Pallas kernels: 0 us -> 65 us
  other arithmetic: 37 us -> 1.31 us
  matrix products: 32 us -> 0 us
  starting transfers between devices: 15.6 us -> 0 us
  between operations: 14.3 us -> 0.67 us
    all_gather x2 -> x0, waiting for transfers between devices: 179 us -> none  [operator(): lax.all_gather(field_z, 'mode', axis=0, tiled=True)]
    pallas_call x0 -> x1, Pallas kernels: none -> 65 us  [body(): pl.pallas_call(functools.partial(kernel, groups, count), out_shape=(whole...]
    dot_general x3 -> x0, matrix products: 32 us -> none  [the longest x2 31.8 us: operator(): jnp.einsum('mij,jzxy->mizxy', rows_here, lax.all_gather(field_z, 'mode',...]
    reduce_sum x2 -> x0, other arithmetic: 29.5 us -> none  [operator(): return jnp.sum(stencil(pad_sides(mixed), coeff_pad[:, None]), axis=0)]
    ppermute x6 -> x0, starting transfers between devices: 15.5 us -> none  [the longest x3 11.6 us: extended(): lax.ppermute(lax.slice_in_dim(block, block.shape[dim] - width, None, axis...]
    ppermute x6 -> x0, waiting for transfers between devices: 8.56 us -> none  [the longest x3 8.37 us: extended(): lax.ppermute(lax.slice_in_dim(block, 0, width, axis=dim), axis, backward)]
    concatenate x5 -> x1, other arithmetic: 3.86 us -> 0.01 us  [body(): table = jnp.concatenate([triples.T.astype(jnp.float32), coef[None]], axis=0)]
    unnamed x14 -> x12, local copies, waits for them, and re-layouts: 2.02 us -> 5.27 us
  transfers between devices with their start and end apart: 8 -> 0, of which waited for: 6 -> 0; matrix products, arithmetic and copies ran while one was open for 1% -> 0% of each run, Pallas kernels for 0% -> 0%
where the time goes in v1:
time: 73.7 us; the launch traced here: 72.4 us
  Pallas kernels  65 us (88%)
  local copies, waits for them, and re-layouts  5.39 us (7%)
  other arithmetic  1.31 us (2%)
    pallas_call x1, Pallas kernels, body(): pl.pallas_call(functools.partial(kernel, groups, count), out_shape=(whole...  65 us
    unnamed x12, local copies, waits for them, and re-layouts  5.27 us

profile of v1, /device:TPU:0, one launch (start us, length us, event | category | flops | bytes accessed | tf_op | source)
XLA Modules:
  0.0 72.4 jit_solution(12567254817536981978)
XLA Ops:
  0.6 0.0 copy-start.4
  0.6 0.7 copy-done.4
  1.3 0.0 copy-start.5
  1.3 0.7 copy-done.5
  2.0 0.0 copy-start
  2.0 1.1 %copy-done = f32[9,2,64,128]{3,2,1,0:T(8,128)S(1)} copy-done((f32[9,2,64,128]{3,2,1,0:T(8,128)S(1)}, f32[9,2,64,128]{3,2,1,0:T(8,128)}, u32[]{:S(2)}) %copy-start) | copy-done | bytes 589848
  3.1 0.0 copy-start.1
  3.1 1.1 %copy-done.1 = f32[9,2,64,128]{3,2,1,0:T(8,128)S(1)} copy-done((f32[9,2,64,128]{3,2,1,0:T(8,128)S(1)}, f32[9,2,64,128]{3,2,1,0:T(8,128)}, u32[]{:S(2)}) %copy-start.1) | copy-done | bytes 589848
  4.1 0.0 copy-start.2
  4.1 0.9 %copy-done.2 = f32[4,2,64,128]{3,2,1,0:T(8,128)S(1)} copy-done((f32[4,2,64,128]{3,2,1,0:T(8,128)S(1)}, f32[4,2,64,128]{3,2,1,0:T(8,128)}, u32[]{:S(2)}) %copy-start.2) | copy-done | bytes 262168
  5.1 0.0 copy-start.3
  5.1 0.8 %copy-done.3 = f32[2,64,128]{2,1,0:T(8,128)S(1)} copy-done((f32[2,64,128]{2,1,0:T(8,128)S(1)}, f32[2,64,128]{2,1,0:T(8,128)}, u32[]{:S(2)}) %copy-start.3) | copy-done | bytes 65560
  5.9 65.0 %sweeps.1 = (f32[9,2,64,128]{3,2,1,0:T(8,128)S(1)}, f32[9,2,64,128]{3,2,1,0:T(8,128)S(1)}, f32[2,64,128]{2,1,0:T(8,128)S(1)}, f32[40,128]{1,0:T(8,128)S(1)}) custom-call(f32[4,156]{1,0:T(4,128)S(1)} %pad_maximum_fusion.table, f32[9,2,64,128]{3,2,1,0:T(8,128)S(1)} %copy-done, f32[9,2,64,128]{3,2,1,0:T(8,128)S(1)} %copy-done.1, f32[2,64,128]{2,1,0:T(8,128)S(1)} %copy-done.3, ...), custom_call_target="tpu_custom_call" | custom-call | tf_op jit(solution)/shard_map/sweeps/pallas_call | solution.py:337
  71.0 0.1 dynamic-slice_reduce_fusion
  71.1 1.3 %fusion.1 = (f32[9,2,64,128]{3,2,1,0:T(8,128)}, f32[9,2,64,128]{3,2,1,0:T(8,128)}) fusion(f32[9,2,64,128]{3,2,1,0:T(8,128)S(1)} %copy-done, f32[9,2,64,128]{3,2,1,0:T(8,128)S(1)} %copy-done.1, f32[9,2,64,128]{3,2,1,0:T(8,128)S(1)} %get-tuple-element.6, f32[2,64,128]{2,1,0:T(8,128)S(1)} %get-tuple-element.8, f32[9]{0:T(128)S(1)} %dynamic-slice_reduce_fusion, ...), kind=kLoop, calls=%fused_computation.3 | loop fusion | flops 1327104 | bytes 3604516 | tf_op jit(solution)/shard_map/add | solution.py:368
  (2 shorter events, 0.0 us)
Async XLA Ops:
  0.6 0.7 copy-start.4
  1.3 0.7 copy-start.5
  2.0 1.1 %copy-start = (f32[9,2,64,128]{3,2,1,0:T(8,128)S(1)}, f32[9,2,64,128]{3,2,1,0:T(8,128)}, u32[]{:S(2)}) copy-start(f32[9,2,64,128]{3,2,1,0:T(8,128)} %start.1) | copy-start | bytes 1769476
  3.1 1.1 %copy-start.1 = (f32[9,2,64,128]{3,2,1,0:T(8,128)S(1)}, f32[9,2,64,128]{3,2,1,0:T(8,128)}, u32[]{:S(2)}) copy-start(f32[9,2,64,128]{3,2,1,0:T(8,128)} %source.1) | copy-start | bytes 1769476
  4.1 0.9 %copy-start.2 = (f32[4,2,64,128]{3,2,1,0:T(8,128)S(1)}, f32[4,2,64,128]{3,2,1,0:T(8,128)}, u32[]{:S(2)}) copy-start(f32[4,2,64,128]{3,2,1,0:T(8,128)} %kl.1) | copy-start | bytes 786436
  5.1 0.8 %copy-start.3 = (f32[2,64,128]{2,1,0:T(8,128)S(1)}, f32[2,64,128]{2,1,0:T(8,128)}, u32[]{:S(2)}) copy-start(f32[2,64,128]{2,1,0:T(8,128)} %mean.1) | copy-start | bytes 196612

commit v2 on v1

--- a/solution.py
+++ b/solution.py
@@ -16,10 +16,10 @@
 
 
 def kernel(
-    groups, count, table, start, source, mean, kl,
+    groups, count, triples, coef, start, source, mean, kl,
     a_first, a_second, total_out, diag_out,
-    coefs, weights, in_first, in_second, out_first, out_second, vt, cmat,
-    trade_send, trade_recv, own_sem, plane_send, plane_recv, row_send, row_recv,
+    triples_here, coef_here, coefs, weights, in_first, in_second, out_first, out_second, vt, cmat,
+    trade_send, trade_recv, own_sem, fetch_sem, plane_send, plane_recv, row_send, row_recv,
 ):
     local, planes, height, lanes = start.shape
     slots = local * groups
@@ -47,10 +47,18 @@
     def _():
         pl.semaphore_signal(barrier, inc=1, device_id={"space": at + 1}, device_id_type=MESH)
 
-    for z in range(planes):
-        coefs[z + 1, 0] = mean[z]
-        for m in range(1, nfields):
-            coefs[z + 1, m] = kl[m - 1, z]
+    fetches = [
+        pltpu.make_async_copy(triples, triples_here, fetch_sem.at[0]),
+        pltpu.make_async_copy(coef, coef_here, fetch_sem.at[1]),
+        pltpu.make_async_copy(mean, coefs.at[pl.ds(1, planes), 0], fetch_sem.at[2]),
+    ] + [
+        pltpu.make_async_copy(
+            kl.at[:, z], coefs.at[z + 1, pl.ds(1, nfields - 1)], fetch_sem.at[3 + z]
+        )
+        for z in range(planes)
+    ]
+    for copy in fetches:
+        copy.start()
 
     @pl.when(jnp.logical_not(has_left))
     def _():
@@ -75,6 +83,12 @@
         for k in range(2):
             for z in range(planes):
                 vt[k, z + 1, rows + 1] = jnp.zeros(vt.shape[3:], jnp.float32)
+
+    far = lax.rem(at, 2)
+    near = 1 - far
+
+    def plane_of(side, i):
+        return side * (planes - 1) + (1 - 2 * side) * i
 
     def band(ref, which):
         return ref.at[:, :, pl.ds(pl.multiple_of(which * rows, rows), rows), :]
@@ -85,14 +99,19 @@
             local, planes, rows, lanes
         )
 
+    def ends(phase, target, owner):
+        if phase == 0:
+            return band(start, target), modes(in_first, owner)
+        if phase == 1:
+            return band(source, target), modes(in_second, owner)
+        if phase == 2:
+            return modes(out_first, target), band(a_first, owner)
+        z = plane_of(near, phase - 3)
+        return modes(out_second, target).at[:, z], band(a_second, owner).at[:, z]
+
     def remote(phase, d):
         peer = lax.rem(me + d, groups)
-        if phase < 2:
-            src = band((start, source)[phase], peer)
-            dst = modes((in_first, in_second)[phase], me)
-        else:
-            src = modes((out_first, out_second)[phase - 2], peer)
-            dst = band((a_first, a_second)[phase - 2], me)
+        src, dst = ends(phase, peer, me)
         return pltpu.make_async_remote_copy(
             src_ref=src, dst_ref=dst,
             send_sem=trade_send.at[phase, d - 1], recv_sem=trade_recv.at[phase, d - 1],
@@ -100,16 +119,13 @@
         )
 
     def own(phase):
-        if phase < 2:
-            src = band((start, source)[phase], me)
-            dst = modes((in_first, in_second)[phase], me)
-        else:
-            src = modes((out_first, out_second)[phase - 2], me)
-            dst = band((a_first, a_second)[phase - 2], me)
+        src, dst = ends(phase, me, me)
         return pltpu.make_async_copy(src, dst, own_sem.at[phase])
 
-    def trade_start(phase):
-        for d in (2, 1, 3) if groups == 4 else range(1, groups):
+    def trade_start(phase, after=None):
+        for d in range(1, groups):
+            if after is not None:
+                remote(after, d).wait_send()
             remote(phase, d).start()
         own(phase).start()
 
@@ -123,31 +139,33 @@
         own(phase).wait()
 
     def plane_copy(k, side):
-        if k == 2:
-            buf, inner = coefs, lambda z: coefs.at[z]
-        else:
-            buf, inner = vt, lambda z: vt.at[k, z, pl.ds(1, rows)]
-        src, dst = (1, planes + 1) if side == 0 else (planes, 0)
+        src, dst = 1 + side * (planes - 1), (planes + 1) * (1 - side)
+        inner = (lambda z: coefs.at[z]) if k == 2 else (lambda z: vt.at[k, z, pl.ds(1, rows)])
         return pltpu.make_async_remote_copy(
             src_ref=inner(src), dst_ref=inner(dst),
             send_sem=plane_send.at[k, side], recv_sem=plane_recv.at[k, side],
-            device_id={"space": at - 1 if side == 0 else at + 1}, device_id_type=MESH,
-        )
+            device_id={"space": at - 1 + 2 * side}, device_id_type=MESH,
+        )
+
+    def has(side):
+        other = at - 1 + 2 * side
+        return jnp.logical_and(other >= 0, other < count)
 
     def plane_start(k, side):
-        @pl.when(has_left if side == 0 else has_right)
+        @pl.when(has(side))
         def _():
             plane_copy(k, side).start()
 
-    def plane_wait(k):
-        for side, sends, gets in ((0, has_left, has_right), (1, has_right, has_left)):
-            @pl.when(sends)
+    def plane_wait_send(k):
+        for side in range(2):
+            @pl.when(has(side))
             def _():
                 plane_copy(k, side).wait_send()
 
-            @pl.when(gets)
-            def _():
-                plane_copy(k, side).wait_recv()
+    def plane_wait_recv(k, side):
+        @pl.when(has(side))
+        def _():
+            plane_copy(k, 1 - side).wait_recv()
 
     has_up = me > 0
     has_down = me < groups - 1
@@ -180,15 +198,17 @@
         barrier, groups - 1 + has_left.astype(jnp.int32) + has_right.astype(jnp.int32)
     )
     trade_start(0)
+    for copy in fetches:
+        copy.wait()
     plane_start(2, 0)
     plane_start(2, 1)
 
-    nnz = table.shape[1]
+    nnz = coef_here.shape[1]
     width = cmat.shape[1]
-    fields_row, rows_row, cols_row, coef_row = (table[i:i + 1, :] for i in range(4))
-    row_hot = lax.broadcasted_iota(jnp.int32, (padded, nnz), 0).astype(jnp.float32) == rows_row
-    key = fields_row * padded + cols_row
-    key_hot = lax.broadcasted_iota(jnp.int32, (width, nnz), 0).astype(jnp.float32) == key
+    fields_row, rows_row, cols_row = (triples_here[i:i + 1, :] for i in range(3))
+    coef_row = coef_here[...]
+    row_hot = lax.broadcasted_iota(jnp.int32, (padded, nnz), 0) == rows_row
+    key_hot = lax.broadcasted_iota(jnp.int32, (width, nnz), 0) == fields_row * padded + cols_row
     coef_high = coef_row.astype(jnp.bfloat16).astype(jnp.float32)
     row_one = jnp.where(row_hot, 1.0, 0.0).astype(jnp.bfloat16)
     for piece, value in enumerate((coef_high, coef_row - coef_high)):
@@ -198,14 +218,15 @@
         )
         cmat[piece * padded:(piece + 1) * padded, :] = part.astype(jnp.bfloat16)
     diag = jnp.sum(
-        jnp.where(jnp.logical_and(row_hot, fields_row == 0.0), coef_row, 0.0), axis=1, keepdims=True
+        jnp.where(jnp.logical_and(row_hot, fields_row == 0), coef_row, 0.0), axis=1, keepdims=True
     )
     real = lax.broadcasted_iota(jnp.int32, (padded, 1), 0) < slots
     diag = jnp.where(real, diag, 1.0)
     diag_out[...] = jnp.broadcast_to(diag, diag_out.shape)
     step = 0.8 / diag
 
-    plane_wait(2)
+    plane_wait_recv(2, 0)
+    plane_wait_recv(2, 1)
     lane = lax.broadcasted_iota(jnp.int32, (height, lanes), 1)
     row = lax.broadcasted_iota(jnp.int32, (height, lanes), 0)
     for z in range(planes):
@@ -228,8 +249,7 @@
                 total_out[z] = total
                 weights[pl.ds(first + (FACES + 1) * nfields, height, stride=entries), :] = 1.0 / total
 
-    trade_wait_send(0)
-    trade_start(1)
+    trade_start(1, after=0)
     trade_wait_recv(0)
 
     fill = jnp.zeros((padded - slots, lanes), jnp.float32)
@@ -242,16 +262,30 @@
         base = pl.multiple_of((z * height + me * rows + y) * entries, 8)
         return weights[pl.ds(base, entries), :]
 
-    for z in range(planes):
-        def relay(y, carry):
-            vt[0, z + 1, y + 1] = jnp.concatenate([fetch(in_first, z, y), fill], axis=0)
+    def fill_field(k, one_row, between):
+        def edges(z, carry):
+            one_row(z, 0)
+            one_row(z, rows - 1)
             return carry
-        lax.fori_loop(0, rows, relay, 0)
-        if z == 0:
-            plane_start(0, 0)
-        if z == planes - 1:
-            plane_start(0, 1)
-    row_start(0)
+        lax.fori_loop(0, planes, edges, 0)
+        row_start(k)
+        between()
+        for i in range(planes):
+            z = plane_of(far, i)
+
+            def inner(y, carry):
+                one_row(z, y)
+                return carry
+            lax.fori_loop(1, rows - 1, inner, 0)
+            if i == 0:
+                plane_start(k, far)
+            if i == planes - 1:
+                plane_start(k, near)
+
+    def relay(z, y):
+        vt[0, z + 1, y + 1] = jnp.concatenate([fetch(in_first, z, y), fill], axis=0)
+
+    fill_field(0, relay, lambda: None)
 
     def applied(k, z, y):
         w = spread_weights(z, y)
@@ -273,50 +307,48 @@
             parts.append(jnp.zeros((width - nfields * padded, lanes), jnp.float32))
         return jnp.concatenate(parts, axis=0)
 
-    def sweep(k, out):
-        def pair(t, carry):
-            z = t // half
-            y = 2 * lax.rem(t, half)
-            x = jnp.concatenate([applied(k, z, y), applied(k, z, y + 1)], axis=1)
-            high = x.astype(jnp.bfloat16)
-            low = (x - high.astype(jnp.float32)).astype(jnp.bfloat16)
-            both = jnp.dot(cmat[...], high, preferred_element_type=jnp.float32)
-            rest = jnp.dot(cmat[:padded, :], low, preferred_element_type=jnp.float32)
-            value = both[:padded] + (both[padded:] + rest)
-            for i in range(2):
-                out[pl.ds(z * rows + y + i, slots, stride=stride), :] = value[
-                    :slots, i * lanes:(i + 1) * lanes
-                ]
-            return carry
-        lax.fori_loop(0, planes * half, pair, 0)
-
-    plane_wait(0)
-    row_wait(0)
-    sweep(0, out_first)
+    def sweep(k, out, done):
+        row_wait(k)
+        for i in range(planes):
+            z = plane_of(near, i)
+            if i == 0:
+                plane_wait_recv(k, near)
+            if i == planes - 1:
+                plane_wait_recv(k, far)
+
+            def pair(t, carry):
+                y = 2 * t
+                x = jnp.concatenate([applied(k, z, y), applied(k, z, y + 1)], axis=1)
+                high = x.astype(jnp.bfloat16)
+                low = (x - high.astype(jnp.float32)).astype(jnp.bfloat16)
+                both = jnp.dot(cmat[...], high, preferred_element_type=jnp.float32)
+                rest = jnp.dot(cmat[:padded, :], low, preferred_element_type=jnp.float32)
+                value = both[:padded] + (both[padded:] + rest)
+                for j in range(2):
+                    out[pl.ds(z * rows + y + j, slots, stride=stride), :] = value[
+                        :slots, j * lanes:(j + 1) * lanes
+                    ]
+                return carry
+            lax.fori_loop(0, half, pair, 0)
+            done(i, z)
+
+    sweep(0, out_first, lambda i, z: None)
     trade_wait_recv(1)
-    trade_wait_send(1)
-
-    for z in range(planes):
-        def update(y, carry):
-            inverse = spread_weights(z, y)[(FACES + 1) * nfields:(FACES + 1) * nfields + 1]
-            first = fetch(in_second, z, y) - fetch(out_first, z, y)
-            first = jnp.concatenate([first, fill], axis=0)
-            vt[1, z + 1, y + 1] = vt[0, z + 1, y + 1] + first * (step * inverse)
-            return carry
-        lax.fori_loop(0, rows, update, 0)
-        if z == 0:
-            plane_start(1, 0)
-        if z == planes - 1:
-            plane_start(1, 1)
-    row_start(1)
-    trade_start(2)
-    plane_wait(1)
-    row_wait(1)
-    sweep(1, out_second)
-    trade_start(3)
-    for phase in (2, 3):
+
+    def update(z, y):
+        inverse = spread_weights(z, y)[(FACES + 1) * nfields:(FACES + 1) * nfields + 1]
+        first = fetch(in_second, z, y) - fetch(out_first, z, y)
+        first = jnp.concatenate([first, fill], axis=0)
+        vt[1, z + 1, y + 1] = vt[0, z + 1, y + 1] + first * (step * inverse)
+
+    fill_field(1, update, lambda: trade_start(2))
+    sweep(1, out_second, lambda i, z: trade_start(3 + i))
+    for k in range(3):
+        plane_wait_send(k)
+    for phase in range(1, 3 + planes):
         trade_wait_send(phase)
-        trade_wait_recv(phase)
+        if phase > 1:
+            trade_wait_recv(phase)
 
 
 def body(count, start_field, source, mean_field, kl_fields, triples, coef):
@@ -328,7 +360,7 @@
     padded = round_up(slots, 8)
     width = round_up(nfields * padded, 16)
     entries = round_up((FACES + 1) * nfields + 1, 8)
-    table = jnp.concatenate([triples.T.astype(jnp.float32), coef[None]], axis=0)
+    nnz = triples.shape[0]
     f32 = jnp.float32
     whole = jax.ShapeDtypeStruct(start_field.shape, f32)
     in_vmem = pl.BlockSpec(memory_space=pltpu.VMEM)
@@ -341,9 +373,11 @@
             jax.ShapeDtypeStruct((planes, height, lanes), f32),
             jax.ShapeDtypeStruct((padded, lanes), f32),
         ),
-        in_specs=[in_vmem, anywhere, anywhere, in_vmem, in_vmem],
+        in_specs=[pl.BlockSpec(memory_space=pltpu.HBM)] * 6,
         out_specs=(anywhere, anywhere, in_vmem, in_vmem),
         scratch_shapes=[
+            pltpu.VMEM((3, nnz), jnp.int32),
+            pltpu.VMEM((1, nnz), f32),
             pltpu.VMEM((planes + 2, nfields, height, lanes), f32),
             pltpu.VMEM((planes * height * entries, lanes), f32),
             pltpu.VMEM((slots * planes * rows, lanes), f32),
@@ -352,14 +386,15 @@
             pltpu.VMEM((slots * planes * rows, lanes), f32),
             pltpu.VMEM((2, planes + 2, rows + 2, padded, lanes), f32),
             pltpu.VMEM((2 * padded, width), jnp.bfloat16),
-            dma((4, groups - 1)), dma((4, groups - 1)), dma((4,)),
+            dma((3 + planes, groups - 1)), dma((3 + planes, groups - 1)), dma((3 + planes,)),
+            dma((3 + planes,)),
             dma((3, 2)), dma((3, 2)), dma((2, 2)), dma((2, 2)),
         ],
         compiler_params=pltpu.CompilerParams(
-            collective_id=0, has_side_effects=True, vmem_limit_bytes=40 * 1024 * 1024
+            collective_id=0, has_side_effects=True, vmem_limit_bytes=62 * 1024 * 1024
         ),
         name="sweeps",
-    )(table, start_field, source, mean_field, kl_fields)
+    )(triples.T, coef[None], start_field, source, mean_field, kl_fields)
     first_slot = lax.axis_index("mode") * local
     own_diag = lax.dynamic_slice_in_dim(diag, first_slot, local)[:, 0]
     scaling = own_diag[:, None, None, None] * totals[None]

time: 73.7 us -> 68.1 us (0.924)
  local copies, waits for them, and re-layouts: 5.39 us -> 0.84 us
  Pallas kernels: 65 us -> 63 us
  other arithmetic: 1.31 us -> 2.6 us
    unnamed x12 -> x4, local copies, waits for them, and re-layouts: 5.27 us -> 0.01 us
    pallas_call x1, Pallas kernels: 65 us -> 63 us  [body(): pl.pallas_call(functools.partial(kernel, groups, count), out_shape=(whole...]
    add x1, other arithmetic: 1.29 us -> 2.6 us  [body(): return (middle + 0.8 * residual / scaling, residual)]
where the time goes in v2:
time: 68.1 us; the launch traced here: 67.1 us
  Pallas kernels  63 us (93%)
  other arithmetic  2.6 us (4%)
  local copies, waits for them, and re-layouts  0.84 us (1%)
    pallas_call x1, Pallas kernels, body(): pl.pallas_call(functools.partial(kernel, groups, count), out_shape=(whole...  63 us
    add x1, other arithmetic, body(): return (middle + 0.8 * residual / scaling, residual)  2.6 us

profile of v2, /device:TPU:0, one launch (start us, length us, event | category | flops | bytes accessed | tf_op | source)
XLA Modules:
  0.0 67.1 jit_solution(15918329938203330909)
XLA Ops:
  0.6 0.0 copy-start
  0.6 0.0 copy-start.1
  0.7 63.0 %sweeps.1 = (f32[9,2,64,128]{3,2,1,0:T(8,128)}, f32[9,2,64,128]{3,2,1,0:T(8,128)}, f32[2,64,128]{2,1,0:T(8,128)}, f32[40,128]{1,0:T(8,128)}) custom-call(s32[3,156]{1,0:T(4,128)} %bitcast.2, f32[1,156]{1,0:T(1,128)} %bitcast.3, f32[9,2,64,128]{3,2,1,0:T(8,128)} %start.1, f32[9,2,64,128]{3,2,1,0:T(8,128)} %source.1, f32[2,64,128]{2,1,0:T(8,128)} %mean.1, ...), custom_call_target="tpu_custom_call" | custom-call | tf_op jit(solution)/shard_map/sweeps/pallas_call | solution.py:369
  63.7 0.8 %dynamic-slice_reduce_fusion = f32[9]{0:T(128)S(1)} fusion(f32[40,128]{1,0:T(8,128)} %get-tuple-element.7, s32[]{:T(128)S(6)} %select_n.3), kind=kLoop, calls=%fused_computation.4 | loop fusion | bytes 76 | tf_op jit(solution)/shard_map/slice | solution.py:399
  64.5 0.0 copy-done
  64.5 0.0 copy-done.1
  64.5 2.6 %fusion.1 = (f32[9,2,64,128]{3,2,1,0:T(8,128)}, f32[9,2,64,128]{3,2,1,0:T(8,128)}) fusion(f32[9,2,64,128]{3,2,1,0:T(8,128)S(1)} %copy-done, f32[9,2,64,128]{3,2,1,0:T(8,128)S(1)} %copy-done.1, f32[9,2,64,128]{3,2,1,0:T(8,128)} %get-tuple-element.6, f32[2,64,128]{2,1,0:T(8,128)} %get-tuple-element.8, f32[9]{0:T(128)S(1)} %dynamic-slice_reduce_fusion, ...), kind=kLoop, calls=%fused_computation.3 | loop fusion | flops 1327104 | bytes 3604516 | tf_op jit(solution)/shard_map/add | solution.py:403
Async XLA Ops:
  0.6 63.9 %copy-start = (f32[9,2,64,128]{3,2,1,0:T(8,128)S(1)}, f32[9,2,64,128]{3,2,1,0:T(8,128)}, u32[]{:S(2)}) copy-start(f32[9,2,64,128]{3,2,1,0:T(8,128)} %start.1) | copy-start | bytes 1769476
  0.6 63.9 %copy-start.1 = (f32[9,2,64,128]{3,2,1,0:T(8,128)S(1)}, f32[9,2,64,128]{3,2,1,0:T(8,128)}, u32[]{:S(2)}) copy-start(f32[9,2,64,128]{3,2,1,0:T(8,128)} %source.1) | copy-start | bytes 1769476

commit v3 on v2

--- a/solution.py
+++ b/solution.py
@@ -99,44 +99,48 @@
             local, planes, rows, lanes
         )
 
-    def ends(phase, target, owner):
-        if phase == 0:
-            return band(start, target), modes(in_first, owner)
-        if phase == 1:
-            return band(source, target), modes(in_second, owner)
-        if phase == 2:
-            return modes(out_first, target), band(a_first, owner)
-        z = plane_of(near, phase - 3)
-        return modes(out_second, target).at[:, z], band(a_second, owner).at[:, z]
-
-    def remote(phase, d):
+    def ends(phase, i, target, owner):
+        if phase < 2:
+            z = plane_of(far, i)
+            return (
+                band((start, source)[phase], target).at[:, z],
+                modes((in_first, in_second)[phase], owner).at[:, z],
+            )
+        z = plane_of(near, i)
+        return (
+            modes((out_first, out_second)[phase - 2], target).at[:, z],
+            band((a_first, a_second)[phase - 2], owner).at[:, z],
+        )
+
+    def remote(phase, i, d):
         peer = lax.rem(me + d, groups)
-        src, dst = ends(phase, peer, me)
+        src, dst = ends(phase, i, peer, me)
+        part = phase * planes + i
         return pltpu.make_async_remote_copy(
             src_ref=src, dst_ref=dst,
-            send_sem=trade_send.at[phase, d - 1], recv_sem=trade_recv.at[phase, d - 1],
+            send_sem=trade_send.at[part, d - 1], recv_sem=trade_recv.at[part, d - 1],
             device_id={"mode": peer}, device_id_type=MESH,
         )
 
-    def own(phase):
-        src, dst = ends(phase, me, me)
-        return pltpu.make_async_copy(src, dst, own_sem.at[phase])
-
-    def trade_start(phase, after=None):
+    def own(phase, i):
+        src, dst = ends(phase, i, me, me)
+        return pltpu.make_async_copy(src, dst, own_sem.at[phase * planes + i])
+
+    def trade_start(phase, i, after=None):
         for d in range(1, groups):
             if after is not None:
-                remote(after, d).wait_send()
-            remote(phase, d).start()
-        own(phase).start()
-
-    def trade_wait_send(phase):
+                remote(*after, d).wait_send()
+            remote(phase, i, d).start()
+        own(phase, i).start()
+
+    def trade_wait_send(phase, i):
         for d in range(1, groups):
-            remote(phase, d).wait_send()
-
-    def trade_wait_recv(phase):
+            remote(phase, i, d).wait_send()
+
+    def trade_wait_recv(phase, i):
         for d in range(1, groups):
-            remote(phase, d).wait_recv()
-        own(phase).wait()
+            remote(phase, i, d).wait_recv()
+        own(phase, i).wait()
 
     def plane_copy(k, side):
         src, dst = 1 + side * (planes - 1), (planes + 1) * (1 - side)
@@ -170,34 +174,36 @@
     has_up = me > 0
     has_down = me < groups - 1
 
-    def row_copy(k, side):
+    def row_copy(k, z, side):
         src, dst = (1, rows + 1) if side == 0 else (rows, 0)
         return pltpu.make_async_remote_copy(
-            src_ref=vt.at[k, pl.ds(1, planes), src], dst_ref=vt.at[k, pl.ds(1, planes), dst],
-            send_sem=row_send.at[k, side], recv_sem=row_recv.at[k, side],
+            src_ref=vt.at[k, z + 1, src], dst_ref=vt.at[k, z + 1, dst],
+            send_sem=row_send.at[k, z, side], recv_sem=row_recv.at[k, z, side],
             device_id={"mode": me - 1 if side == 0 else me + 1}, device_id_type=MESH,
         )
 
-    def row_start(k):
+    def row_start(k, z):
         for side, sends in ((0, has_up), (1, has_down)):
             @pl.when(sends)
             def _():
-                row_copy(k, side).start()
-
-    def row_wait(k):
-        for side, sends, gets in ((0, has_up, has_down), (1, has_down, has_up)):
+                row_copy(k, z, side).start()
+
+    def row_wait_send(k, z):
+        for side, sends in ((0, has_up), (1, has_down)):
             @pl.when(sends)
             def _():
-                row_copy(k, side).wait_send()
-
+                row_copy(k, z, side).wait_send()
+
+    def row_wait_recv(k, z):
+        for side, gets in ((0, has_down), (1, has_up)):
             @pl.when(gets)
             def _():
-                row_copy(k, side).wait_recv()
+                row_copy(k, z, side).wait_recv()
 
     pl.semaphore_wait(
         barrier, groups - 1 + has_left.astype(jnp.int32) + has_right.astype(jnp.int32)
     )
-    trade_start(0)
+    trade_start(0, 0)
     for copy in fetches:
         copy.wait()
     plane_start(2, 0)
@@ -222,8 +228,44 @@
     )
     real = lax.broadcasted_iota(jnp.int32, (padded, 1), 0) < slots
     diag = jnp.where(real, diag, 1.0)
-    diag_out[...] = jnp.broadcast_to(diag, diag_out.shape)
+    own_hot = lax.broadcasted_iota(jnp.int32, (diag_out.shape[0], nnz), 0) + me * local == rows_row
+    own_diag = jnp.sum(
+        jnp.where(jnp.logical_and(own_hot, fields_row == 0), coef_row, 0.0), axis=1, keepdims=True
+    )
+    diag_out[...] = jnp.broadcast_to(own_diag, diag_out.shape)
     step = 0.8 / diag
+
+    fill = jnp.zeros((padded - slots, lanes), jnp.float32)
+
+    def fetch(ref, z, y):
+        return ref[pl.ds(z * rows + y, slots, stride=stride), :]
+
+    def spread_weights(z, y):
+        base = pl.multiple_of((z * height + me * rows + y) * entries, 8)
+        return weights[pl.ds(base, entries), :]
+
+    def fill_plane(k, i, one_row):
+        z = plane_of(far, i)
+        one_row(z, 0)
+        one_row(z, rows - 1)
+        row_start(k, z)
+
+        def inner(y, carry):
+            one_row(z, y)
+            return carry
+        lax.fori_loop(1, rows - 1, inner, 0)
+        if i == 0:
+            plane_start(k, far)
+        if i == planes - 1:
+            plane_start(k, near)
+
+    def relay(z, y):
+        vt[0, z + 1, y + 1] = jnp.concatenate([fetch(in_first, z, y), fill], axis=0)
+
+    for i in range(planes - 1):
+        trade_start(0, i + 1, after=(0, i))
+        trade_wait_recv(0, i)
+        fill_plane(0, i, relay)
 
     plane_wait_recv(2, 0)
     plane_wait_recv(2, 1)
@@ -249,43 +291,10 @@
                 total_out[z] = total
                 weights[pl.ds(first + (FACES + 1) * nfields, height, stride=entries), :] = 1.0 / total
 
-    trade_start(1, after=0)
-    trade_wait_recv(0)
-
-    fill = jnp.zeros((padded - slots, lanes), jnp.float32)
-    half = rows // 2
-
-    def fetch(ref, z, y):
-        return ref[pl.ds(z * rows + y, slots, stride=stride), :]
-
-    def spread_weights(z, y):
-        base = pl.multiple_of((z * height + me * rows + y) * entries, 8)
-        return weights[pl.ds(base, entries), :]
-
-    def fill_field(k, one_row, between):
-        def edges(z, carry):
-            one_row(z, 0)
-            one_row(z, rows - 1)
-            return carry
-        lax.fori_loop(0, planes, edges, 0)
-        row_start(k)
-        between()
-        for i in range(planes):
-            z = plane_of(far, i)
-
-            def inner(y, carry):
-                one_row(z, y)
-                return carry
-            lax.fori_loop(1, rows - 1, inner, 0)
-            if i == 0:
-                plane_start(k, far)
-            if i == planes - 1:
-                plane_start(k, near)
-
-    def relay(z, y):
-        vt[0, z + 1, y + 1] = jnp.concatenate([fetch(in_first, z, y), fill], axis=0)
-
-    fill_field(0, relay, lambda: None)
+    last = planes - 1
+    trade_start(1, 0, after=(0, last))
+    trade_wait_recv(0, last)
+    fill_plane(0, last, relay)
 
     def applied(k, z, y):
         w = spread_weights(z, y)
@@ -307,33 +316,36 @@
             parts.append(jnp.zeros((width - nfields * padded, lanes), jnp.float32))
         return jnp.concatenate(parts, axis=0)
 
-    def sweep(k, out, done):
-        row_wait(k)
-        for i in range(planes):
-            z = plane_of(near, i)
-            if i == 0:
-                plane_wait_recv(k, near)
-            if i == planes - 1:
-                plane_wait_recv(k, far)
-
-            def pair(t, carry):
-                y = 2 * t
-                x = jnp.concatenate([applied(k, z, y), applied(k, z, y + 1)], axis=1)
-                high = x.astype(jnp.bfloat16)
-                low = (x - high.astype(jnp.float32)).astype(jnp.bfloat16)
-                both = jnp.dot(cmat[...], high, preferred_element_type=jnp.float32)
-                rest = jnp.dot(cmat[:padded, :], low, preferred_element_type=jnp.float32)
-                value = both[:padded] + (both[padded:] + rest)
-                for j in range(2):
-                    out[pl.ds(z * rows + y + j, slots, stride=stride), :] = value[
-                        :slots, j * lanes:(j + 1) * lanes
-                    ]
-                return carry
-            lax.fori_loop(0, half, pair, 0)
-            done(i, z)
-
-    sweep(0, out_first, lambda i, z: None)
-    trade_wait_recv(1)
+    def product(k, z, y):
+        x = jnp.concatenate([applied(k, z, y), applied(k, z, y + 1)], axis=1)
+        high = x.astype(jnp.bfloat16)
+        low = (x - high.astype(jnp.float32)).astype(jnp.bfloat16)
+        both = jnp.dot(cmat[...], high, preferred_element_type=jnp.float32)
+        rest = jnp.dot(cmat[:padded, :], low, preferred_element_type=jnp.float32)
+        return both[:padded] + (both[padded:] + rest)
+
+    def sweep(k, i, out):
+        z = plane_of(near, i)
+        row_wait_recv(k, z)
+        if i == 0:
+            plane_wait_recv(k, near)
+        if i == last:
+            plane_wait_recv(k, far)
+
+        def group(t, carry):
+            y = 4 * t
+            values = [product(k, z, y), product(k, z, y + 2)]
+            for j in range(4):
+                out[pl.ds(z * rows + y + j, slots, stride=stride), :] = values[j // 2][
+                    :slots, (j % 2) * lanes:(j % 2 + 1) * lanes
+                ]
+            return carry
+        lax.fori_loop(0, rows // 4, group, 0)
+
+    for i in range(planes):
+        sweep(0, i, out_first)
+        if i < last:
+            trade_start(1, i + 1, after=(1, i))
 
     def update(z, y):
         inverse = spread_weights(z, y)[(FACES + 1) * nfields:(FACES + 1) * nfields + 1]
@@ -341,14 +353,25 @@
         first = jnp.concatenate([first, fill], axis=0)
         vt[1, z + 1, y + 1] = vt[0, z + 1, y + 1] + first * (step * inverse)
 
-    fill_field(1, update, lambda: trade_start(2))
-    sweep(1, out_second, lambda i, z: trade_start(3 + i))
+    for i in range(planes):
+        if i == last:
+            trade_start(2, 0, after=(1, last))
+        trade_wait_recv(1, i)
+        fill_plane(1, i, update)
+    for i in range(1, planes):
+        trade_start(2, i)
+    for i in range(planes):
+        sweep(1, i, out_second)
+        trade_start(3, i)
     for k in range(3):
         plane_wait_send(k)
-    for phase in range(1, 3 + planes):
-        trade_wait_send(phase)
-        if phase > 1:
-            trade_wait_recv(phase)
+        if k < 2:
+            for z in range(planes):
+                row_wait_send(k, z)
+    for phase in (2, 3):
+        for i in range(planes):
+            trade_wait_send(phase, i)
+            trade_wait_recv(phase, i)
 
 
 def body(count, start_field, source, mean_field, kl_fields, triples, coef):
@@ -371,7 +394,7 @@
         out_shape=(
             whole, whole,
             jax.ShapeDtypeStruct((planes, height, lanes), f32),
-            jax.ShapeDtypeStruct((padded, lanes), f32),
+            jax.ShapeDtypeStruct((round_up(local, 8), lanes), f32),
         ),
         in_specs=[pl.BlockSpec(memory_space=pltpu.HBM)] * 6,
         out_specs=(anywhere, anywhere, in_vmem, in_vmem),
@@ -386,18 +409,16 @@
             pltpu.VMEM((slots * planes * rows, lanes), f32),
             pltpu.VMEM((2, planes + 2, rows + 2, padded, lanes), f32),
             pltpu.VMEM((2 * padded, width), jnp.bfloat16),
-            dma((3 + planes, groups - 1)), dma((3 + planes, groups - 1)), dma((3 + planes,)),
+            dma((4 * planes, groups - 1)), dma((4 * planes, groups - 1)), dma((4 * planes,)),
             dma((3 + planes,)),
-            dma((3, 2)), dma((3, 2)), dma((2, 2)), dma((2, 2)),
+            dma((3, 2)), dma((3, 2)), dma((2, planes, 2)), dma((2, planes, 2)),
         ],
         compiler_params=pltpu.CompilerParams(
             collective_id=0, has_side_effects=True, vmem_limit_bytes=62 * 1024 * 1024
         ),
         name="sweeps",
     )(triples.T, coef[None], start_field, source, mean_field, kl_fields)
-    first_slot = lax.axis_index("mode") * local
-    own_diag = lax.dynamic_slice_in_dim(diag, first_slot, local)[:, 0]
-    scaling = own_diag[:, None, None, None] * totals[None]
+    scaling = diag[:local, None, None, :] * totals[None]
     middle = start_field + 0.8 * (source - a_first) / scaling
     residual = source - a_second
     return middle + 0.8 * residual / scaling, residual

time: 68.1 us -> 66.5 us (0.977); the launches traced: 67.1 us -> 66.3 us
    slice x1 -> x0, local copies, waits for them, and re-layouts: 0.83 us -> none  [body(): own_diag = lax.dynamic_slice_in_dim(diag, first_slot, local)[:, 0]]
where the time goes in v3:
time: 66.5 us; the launch traced here: 66.3 us
  Pallas kernels  62.4 us (94%)
  other arithmetic  2.61 us (4%)
  local copies, waits for them, and re-layouts  0.68 us (1%)
  between operations  0.68 us (1%)
    pallas_call x1, Pallas kernels, body(): pl.pallas_call(functools.partial(kernel, groups, count), out_shape=(whole...  62.4 us
    add x1, other arithmetic, body(): return (middle + 0.8 * residual / scaling, residual)  2.61 us

profile of v3, /device:TPU:0, one launch (start us, length us, event | category | flops | bytes accessed | tf_op | source)
XLA Modules:
  0.0 66.3 jit_solution(17415931354615772947)
XLA Ops:
  0.6 0.0 copy-start
  0.6 0.0 copy-start.1
  0.7 62.4 %sweeps.1 = (f32[9,2,64,128]{3,2,1,0:T(8,128)}, f32[9,2,64,128]{3,2,1,0:T(8,128)}, f32[2,64,128]{2,1,0:T(8,128)}, f32[16,128]{1,0:T(8,128)}) custom-call(s32[3,156]{1,0:T(4,128)} %bitcast.4, f32[1,156]{1,0:T(1,128)} %bitcast.5, f32[9,2,64,128]{3,2,1,0:T(8,128)} %start.1, f32[9,2,64,128]{3,2,1,0:T(8,128)} %source.1, f32[2,64,128]{2,1,0:T(8,128)} %mean.1, ...), custom_call_target="tpu_custom_call" | custom-call | tf_op jit(solution)/shard_map/sweeps/pallas_call | solution.py:392
  63.0 0.0 copy-start.2
  63.0 0.0 copy-done
  63.0 0.0 copy-done.1
  63.1 0.7 %copy-done.2 = f32[16,128]{1,0:T(8,128)S(1)} copy-done((f32[16,128]{1,0:T(8,128)S(1)}, f32[16,128]{1,0:T(8,128)}, u32[]{:S(2)}) %copy-start.2) | copy-done | bytes 8216
  63.7 2.6 %fusion.1 = (f32[9,2,64,128]{3,2,1,0:T(8,128)}, f32[9,2,64,128]{3,2,1,0:T(8,128)}) fusion(f32[9,2,64,128]{3,2,1,0:T(8,128)S(1)} %copy-done, f32[9,2,64,128]{3,2,1,0:T(8,128)S(1)} %copy-done.1, f32[9,2,64,128]{3,2,1,0:T(8,128)} %get-tuple-element.6, f32[2,64,128]{2,1,0:T(8,128)} %get-tuple-element.8, f32[9,128]{1,0:T(8,128)S(1)} %bitcast.3, ...), kind=kLoop, calls=%fused_computation.3 | loop fusion | flops 1327104 | bytes 3609088 | tf_op jit(solution)/shard_map/add | solution.py:424
Async XLA Ops:
  0.6 62.4 %copy-start = (f32[9,2,64,128]{3,2,1,0:T(8,128)S(1)}, f32[9,2,64,128]{3,2,1,0:T(8,128)}, u32[]{:S(2)}) copy-start(f32[9,2,64,128]{3,2,1,0:T(8,128)} %start.1) | copy-start | bytes 1769476
  0.6 62.4 %copy-start.1 = (f32[9,2,64,128]{3,2,1,0:T(8,128)S(1)}, f32[9,2,64,128]{3,2,1,0:T(8,128)}, u32[]{:S(2)}) copy-start(f32[9,2,64,128]{3,2,1,0:T(8,128)} %source.1) | copy-start | bytes 1769476
  63.0 0.7 %copy-start.2 = (f32[16,128]{1,0:T(8,128)S(1)}, f32[16,128]{1,0:T(8,128)}, u32[]{:S(2)}) copy-start(f32[16,128]{1,0:T(8,128)} %get-tuple-element.7) | copy-start | bytes 24580

commit v4 on v3

--- a/solution.py
+++ b/solution.py
@@ -17,9 +17,10 @@
 
 def kernel(
     groups, count, triples, coef, start, source, mean, kl,
-    a_first, a_second, total_out, diag_out,
+    smoothed_out, residual_out,
+    start_here, source_here, a_first, a_second, inverse_total, own_step,
     triples_here, coef_here, coefs, weights, in_first, in_second, out_first, out_second, vt, cmat,
-    trade_send, trade_recv, own_sem, fetch_sem, plane_send, plane_recv, row_send, row_recv,
+    trade_send, trade_recv, own_sem, fetch_sem, home_sem, out_sem, plane_send, plane_recv, row_send, row_recv,
 ):
     local, planes, height, lanes = start.shape
     slots = local * groups
@@ -47,6 +48,10 @@
     def _():
         pl.semaphore_signal(barrier, inc=1, device_id={"space": at + 1}, device_id_type=MESH)
 
+    fields_here = [
+        pltpu.make_async_copy(start, start_here, home_sem.at[0]),
+        pltpu.make_async_copy(source, source_here, home_sem.at[1]),
+    ]
     fetches = [
         pltpu.make_async_copy(triples, triples_here, fetch_sem.at[0]),
         pltpu.make_async_copy(coef, coef_here, fetch_sem.at[1]),
@@ -206,6 +211,8 @@
     trade_start(0, 0)
     for copy in fetches:
         copy.wait()
+    for copy in fields_here:
+        copy.start()
     plane_start(2, 0)
     plane_start(2, 1)
 
@@ -228,11 +235,13 @@
     )
     real = lax.broadcasted_iota(jnp.int32, (padded, 1), 0) < slots
     diag = jnp.where(real, diag, 1.0)
-    own_hot = lax.broadcasted_iota(jnp.int32, (diag_out.shape[0], nnz), 0) + me * local == rows_row
+    own_ids = lax.broadcasted_iota(jnp.int32, (own_step.shape[0], nnz), 0)
     own_diag = jnp.sum(
-        jnp.where(jnp.logical_and(own_hot, fields_row == 0), coef_row, 0.0), axis=1, keepdims=True
+        jnp.where(jnp.logical_and(own_ids + me * local == rows_row, fields_row == 0), coef_row, 0.0),
+        axis=1, keepdims=True,
     )
-    diag_out[...] = jnp.broadcast_to(own_diag, diag_out.shape)
+    own_diag = jnp.where(own_ids[:, :1] < local, own_diag, 1.0)
+    own_step[...] = jnp.broadcast_to(0.8 / own_diag, own_step.shape)
     step = 0.8 / diag
 
     fill = jnp.zeros((padded - slots, lanes), jnp.float32)
@@ -288,8 +297,10 @@
             for f, value in enumerate(faces + [total]):
                 weights[pl.ds(first + f * nfields + m, height, stride=entries), :] = value
             if m == 0:
-                total_out[z] = total
-                weights[pl.ds(first + (FACES + 1) * nfields, height, stride=entries), :] = 1.0 / total
+                inverse_total[z] = 1.0 / total
+                weights[pl.ds(first + (FACES + 1) * nfields, height, stride=entries), :] = (
+                    inverse_total[z]
+                )
 
     last = planes - 1
     trade_start(1, 0, after=(0, last))
@@ -363,6 +374,40 @@
     for i in range(planes):
         sweep(1, i, out_second)
         trade_start(3, i)
+
+    for copy in fields_here:
+        copy.wait()
+    for i in range(planes):
+        trade_wait_recv(2, i)
+
+    def make_middle(j, carry):
+        gain = own_step[pl.ds(j, 1), :]
+        for z in range(planes):
+            first = source_here[j, z] - a_first[j, z]
+            start_here[j, z] = start_here[j, z] + first * (gain * inverse_total[z])
+        return carry
+    lax.fori_loop(0, local, make_middle, 0)
+
+    def results(i):
+        z = plane_of(near, i)
+        return [
+            pltpu.make_async_copy(held.at[:, z], out.at[:, z], out_sem.at[i, n])
+            for n, (held, out) in enumerate(((start_here, smoothed_out), (a_second, residual_out)))
+        ]
+
+    for i in range(planes):
+        z = plane_of(near, i)
+        trade_wait_recv(3, i)
+
+        def make_outputs(j, carry):
+            residual = source_here[j, z] - a_second[j, z]
+            a_second[j, z] = residual
+            gain = own_step[pl.ds(j, 1), :] * inverse_total[z]
+            start_here[j, z] = start_here[j, z] + residual * gain
+            return carry
+        lax.fori_loop(0, local, make_outputs, 0)
+        for copy in results(i):
+            copy.start()
     for k in range(3):
         plane_wait_send(k)
         if k < 2:
@@ -371,7 +416,9 @@
     for phase in (2, 3):
         for i in range(planes):
             trade_wait_send(phase, i)
-            trade_wait_recv(phase, i)
+    for i in range(planes):
+        for copy in results(i):
+            copy.wait()
 
 
 def body(count, start_field, source, mean_field, kl_fields, triples, coef):
@@ -386,19 +433,17 @@
     nnz = triples.shape[0]
     f32 = jnp.float32
     whole = jax.ShapeDtypeStruct(start_field.shape, f32)
-    in_vmem = pl.BlockSpec(memory_space=pltpu.VMEM)
     anywhere = pl.BlockSpec(memory_space=pl.ANY)
     dma = pltpu.SemaphoreType.DMA
-    a_first, a_second, totals, diag = pl.pallas_call(
+    smoothed, residual = pl.pallas_call(
         functools.partial(kernel, groups, count),
-        out_shape=(
-            whole, whole,
-            jax.ShapeDtypeStruct((planes, height, lanes), f32),
-            jax.ShapeDtypeStruct((round_up(local, 8), lanes), f32),
-        ),
+        out_shape=(whole, whole),
         in_specs=[pl.BlockSpec(memory_space=pltpu.HBM)] * 6,
-        out_specs=(anywhere, anywhere, in_vmem, in_vmem),
+        out_specs=(anywhere, anywhere),
         scratch_shapes=[
+            *[pltpu.VMEM(start_field.shape, f32)] * 4,
+            pltpu.VMEM((planes, height, lanes), f32),
+            pltpu.VMEM((round_up(local, 8), lanes), f32),
             pltpu.VMEM((3, nnz), jnp.int32),
             pltpu.VMEM((1, nnz), f32),
             pltpu.VMEM((planes + 2, nfields, height, lanes), f32),
@@ -410,7 +455,7 @@
             pltpu.VMEM((2, planes + 2, rows + 2, padded, lanes), f32),
             pltpu.VMEM((2 * padded, width), jnp.bfloat16),
             dma((4 * planes, groups - 1)), dma((4 * planes, groups - 1)), dma((4 * planes,)),
-            dma((3 + planes,)),
+            dma((3 + planes,)), dma((2,)), dma((planes, 2)),
             dma((3, 2)), dma((3, 2)), dma((2, planes, 2)), dma((2, planes, 2)),
         ],
         compiler_params=pltpu.CompilerParams(
@@ -418,10 +463,7 @@
         ),
         name="sweeps",
     )(triples.T, coef[None], start_field, source, mean_field, kl_fields)
-    scaling = diag[:local, None, None, :] * totals[None]
-    middle = start_field + 0.8 * (source - a_first) / scaling
-    residual = source - a_second
-    return middle + 0.8 * residual / scaling, residual
+    return smoothed, residual
 
 
 def solution(mesh):

time: 66.5 us -> 66.2 us (level)
  other arithmetic: 2.61 us -> 0 us
  local copies, waits for them, and re-layouts: 0.68 us -> 2.81 us
    add x1 -> x0, other arithmetic: 2.61 us -> none  [body(): return (middle + 0.8 * residual / scaling, residual)]
    unnamed x6 -> x4, local copies, waits for them, and re-layouts: 0.68 us -> 2.81 us
where the time goes in v4:
time: 66.2 us; the launch traced here: 66 us
  Pallas kernels  62.6 us (95%)
  local copies, waits for them, and re-layouts  2.81 us (4%)
    pallas_call x1, Pallas kernels, body(): pl.pallas_call(functools.partial(kernel, groups, count), out_shape=(whole...  62.6 us
    unnamed x4, local copies, waits for them, and re-layouts  2.81 us

profile of v4, /device:TPU:0, one launch (start us, length us, event | category | flops | bytes accessed | tf_op | source)
XLA Modules:
  0.0 66.0 jit_solution(7873598653470217163)
XLA Ops:
  0.6 62.6 %sweeps.1 = (f32[9,2,64,128]{3,2,1,0:T(8,128)}, f32[9,2,64,128]{3,2,1,0:T(8,128)}) custom-call(s32[3,156]{1,0:T(4,128)} %bitcast.2, f32[1,156]{1,0:T(1,128)} %bitcast.3, f32[9,2,64,128]{3,2,1,0:T(8,128)} %start.1, f32[9,2,64,128]{3,2,1,0:T(8,128)} %source.1, f32[2,64,128]{2,1,0:T(8,128)} %mean.1, f32[4,2,64,128]{3,2,1,0:T(8,128)} %kl.1), custom_call_target="tpu_custom_call" | custom-call | tf_op jit(solution)/shard_map/sweeps/pallas_call | solution.py:438
  63.2 0.0 copy-start
  63.2 2.0 %copy.10 = f32[9,2,64,128]{3,2,1,0:T(8,128)} copy(f32[9,2,64,128]{3,2,1,0:T(8,128)} %get-tuple-element.4) | data formatting | bytes 1179648
  65.2 0.0 copy-done
  65.2 0.8 %copy.11 = f32[9,2,64,128]{3,2,1,0:T(8,128)} copy(f32[9,2,64,128]{3,2,1,0:T(8,128)S(1)} %copy-done) | data formatting | bytes 1179648
Async XLA Ops:
  63.2 2.0 %copy-start = (f32[9,2,64,128]{3,2,1,0:T(8,128)S(1)}, f32[9,2,64,128]{3,2,1,0:T(8,128)}, u32[]{:S(2)}) copy-start(f32[9,2,64,128]{3,2,1,0:T(8,128)} %get-tuple-element.5) | copy-start | bytes 1769476

commit v5 on v4

--- a/solution.py
+++ b/solution.py
@@ -271,10 +271,8 @@
     def relay(z, y):
         vt[0, z + 1, y + 1] = jnp.concatenate([fetch(in_first, z, y), fill], axis=0)
 
-    for i in range(planes - 1):
-        trade_start(0, i + 1, after=(0, i))
-        trade_wait_recv(0, i)
-        fill_plane(0, i, relay)
+    for i in range(1, planes):
+        trade_start(0, i)
 
     plane_wait_recv(2, 0)
     plane_wait_recv(2, 1)
@@ -303,9 +301,10 @@
                 )
 
     last = planes - 1
-    trade_start(1, 0, after=(0, last))
-    trade_wait_recv(0, last)
-    fill_plane(0, last, relay)
+    for i in range(planes):
+        trade_wait_recv(0, i)
+        fill_plane(0, i, relay)
+        trade_start(1, i, after=(0, i))
 
     def applied(k, z, y):
         w = spread_weights(z, y)
@@ -335,28 +334,33 @@
         rest = jnp.dot(cmat[:padded, :], low, preferred_element_type=jnp.float32)
         return both[:padded] + (both[padded:] + rest)
 
-    def sweep(k, i, out):
+    def sweep(k, i, out, first_group, groups_here, step_here):
         z = plane_of(near, i)
-        row_wait_recv(k, z)
-        if i == 0:
-            plane_wait_recv(k, near)
-        if i == last:
-            plane_wait_recv(k, far)
 
         def group(t, carry):
-            y = 4 * t
+            y = 4 * (first_group + step_here * t)
             values = [product(k, z, y), product(k, z, y + 2)]
             for j in range(4):
                 out[pl.ds(z * rows + y + j, slots, stride=stride), :] = values[j // 2][
                     :slots, (j % 2) * lanes:(j % 2 + 1) * lanes
                 ]
             return carry
-        lax.fori_loop(0, rows // 4, group, 0)
-
-    for i in range(planes):
-        sweep(0, i, out_first)
-        if i < last:
-            trade_start(1, i + 1, after=(1, i))
+        lax.fori_loop(0, groups_here, group, 0)
+
+    def sweep_all(k, out, done):
+        quads = rows // 4
+        for i in range(planes):
+            if i == 0:
+                plane_wait_recv(k, near)
+            if i == last:
+                plane_wait_recv(k, far)
+            sweep(k, i, out, 1, quads - 2, 1)
+        for i in range(planes):
+            row_wait_recv(k, plane_of(near, i))
+            sweep(k, i, out, 0, 2, quads - 1)
+            done(i)
+
+    sweep_all(0, out_first, lambda i: None)
 
     def update(z, y):
         inverse = spread_weights(z, y)[(FACES + 1) * nfields:(FACES + 1) * nfields + 1]
@@ -365,15 +369,10 @@
         vt[1, z + 1, y + 1] = vt[0, z + 1, y + 1] + first * (step * inverse)
 
     for i in range(planes):
-        if i == last:
-            trade_start(2, 0, after=(1, last))
         trade_wait_recv(1, i)
         fill_plane(1, i, update)
-    for i in range(1, planes):
-        trade_start(2, i)
-    for i in range(planes):
-        sweep(1, i, out_second)
-        trade_start(3, i)
+        trade_start(2, i, after=(1, i))
+    sweep_all(1, out_second, lambda i: trade_start(3, i))
 
     for copy in fields_here:
         copy.wait()

time: 66.2 us -> 63.8 us (0.964)
  Pallas kernels: 62.6 us -> 60.2 us
    pallas_call x1, Pallas kernels: 62.6 us -> 60.2 us  [body(): pl.pallas_call(functools.partial(kernel, groups, count), out_shape=(whole...]
where the time goes in v5:
time: 63.8 us; the launch traced here: 63.7 us
  Pallas kernels  60.2 us (94%)
  local copies, waits for them, and re-layouts  2.81 us (4%)
  between operations  0.65 us (1%)
    pallas_call x1, Pallas kernels, body(): pl.pallas_call(functools.partial(kernel, groups, count), out_shape=(whole...  60.2 us
    unnamed x4, local copies, waits for them, and re-layouts  2.81 us

profile of v5, /device:TPU:0, one launch (start us, length us, event | category | flops | bytes accessed | tf_op | source)
XLA Modules:
  0.0 63.7 jit_solution(611053177647830999)
XLA Ops:
  0.6 60.2 %sweeps.1 = (f32[9,2,64,128]{3,2,1,0:T(8,128)}, f32[9,2,64,128]{3,2,1,0:T(8,128)}) custom-call(s32[3,156]{1,0:T(4,128)} %bitcast.2, f32[1,156]{1,0:T(1,128)} %bitcast.3, f32[9,2,64,128]{3,2,1,0:T(8,128)} %start.1, f32[9,2,64,128]{3,2,1,0:T(8,128)} %source.1, f32[2,64,128]{2,1,0:T(8,128)} %mean.1, f32[4,2,64,128]{3,2,1,0:T(8,128)} %kl.1), custom_call_target="tpu_custom_call" | custom-call | tf_op jit(solution)/shard_map/sweeps/pallas_call | solution.py:437
  60.8 0.0 copy-start
  60.8 2.0 %copy.10 = f32[9,2,64,128]{3,2,1,0:T(8,128)} copy(f32[9,2,64,128]{3,2,1,0:T(8,128)} %get-tuple-element.4) | data formatting | bytes 1179648
  62.8 0.0 copy-done
  62.8 0.8 %copy.11 = f32[9,2,64,128]{3,2,1,0:T(8,128)} copy(f32[9,2,64,128]{3,2,1,0:T(8,128)S(1)} %copy-done) | data formatting | bytes 1179648
Async XLA Ops:
  60.8 2.0 %copy-start = (f32[9,2,64,128]{3,2,1,0:T(8,128)S(1)}, f32[9,2,64,128]{3,2,1,0:T(8,128)}, u32[]{:S(2)}) copy-start(f32[9,2,64,128]{3,2,1,0:T(8,128)} %get-tuple-element.5) | copy-start | bytes 1769476

commit v6 on v5

--- a/solution.py
+++ b/solution.py
@@ -302,9 +302,9 @@
 
     last = planes - 1
     for i in range(planes):
+        trade_start(1, i, after=(0, i))
         trade_wait_recv(0, i)
         fill_plane(0, i, relay)
-        trade_start(1, i, after=(0, i))
 
     def applied(k, z, y):
         w = spread_weights(z, y)
@@ -369,9 +369,12 @@
         vt[1, z + 1, y + 1] = vt[0, z + 1, y + 1] + first * (step * inverse)
 
     for i in range(planes):
+        if i == 0:
+            trade_start(2, i, after=(1, i))
         trade_wait_recv(1, i)
         fill_plane(1, i, update)
-        trade_start(2, i, after=(1, i))
+        if i > 0:
+            trade_start(2, i, after=(1, i))
     sweep_all(1, out_second, lambda i: trade_start(3, i))
 
     for copy in fields_here:
@@ -418,6 +421,18 @@
     for i in range(planes):
         for copy in results(i):
             copy.wait()
+
+
+def place(smoothed, residual, smoothed_out, residual_out, sem):
+    copies = [
+        pltpu.make_async_copy(ref.at[j], out.at[j], sem.at[n, j])
+        for n, (ref, out) in enumerate(((smoothed, smoothed_out), (residual, residual_out)))
+        for j in range(ref.shape[0])
+    ]
+    for copy in copies:
+        copy.start()
+    for copy in copies:
+        copy.wait()
 
 
 def body(count, start_field, source, mean_field, kl_fields, triples, coef):
@@ -462,7 +477,15 @@
         ),
         name="sweeps",
     )(triples.T, coef[None], start_field, source, mean_field, kl_fields)
-    return smoothed, residual
+    return pl.pallas_call(
+        place,
+        out_shape=(whole, whole),
+        in_specs=[anywhere, anywhere],
+        out_specs=(anywhere, anywhere),
+        scratch_shapes=[dma((2, local))],
+        compiler_params=pltpu.CompilerParams(vmem_limit_bytes=62 * 1024 * 1024),
+        name="place",
+    )(smoothed, residual)
 
 
 def solution(mesh):

time: 63.8 us -> 98.9 us (1.55)
  Pallas kernels: 60.2 us -> 98.1 us
  local copies, waits for them, and re-layouts: 2.81 us -> 0 us
    pallas_call x0 -> x1, Pallas kernels: none -> 37 us  [body(): pl.pallas_call(place, out_shape=(whole, whole), in_specs=[anywhere, anywh...]
    unnamed x4 -> x0, local copies, waits for them, and re-layouts: 2.81 us -> none
where the time goes in v6:
time: 98.9 us; the launch traced here: 98.7 us
  Pallas kernels  98.1 us (99%)
    pallas_call x1, Pallas kernels, body(): pl.pallas_call(functools.partial(kernel, groups, count), out_shape=(whole...  61.1 us
    pallas_call x1, Pallas kernels, body(): pl.pallas_call(place, out_shape=(whole, whole), in_specs=[anywhere, anywh...  37 us

profile of v6, /device:TPU:0, one launch (start us, length us, event | category | flops | bytes accessed | tf_op | source)
XLA Modules:
  0.0 98.7 jit_solution(8744418005878397473)
XLA Ops:
  0.6 61.1 %sweeps.1 = (f32[9,2,64,128]{3,2,1,0:T(8,128)}, f32[9,2,64,128]{3,2,1,0:T(8,128)}) custom-call(s32[3,156]{1,0:T(4,128)} %bitcast.2, f32[1,156]{1,0:T(1,128)} %bitcast.3, f32[9,2,64,128]{3,2,1,0:T(8,128)} %start.1, f32[9,2,64,128]{3,2,1,0:T(8,128)} %source.1, f32[2,64,128]{2,1,0:T(8,128)} %mean.1, f32[4,2,64,128]{3,2,1,0:T(8,128)} %kl.1), custom_call_target="tpu_custom_call" | custom-call | tf_op jit(solution)/shard_map/sweeps/pallas_call | solution.py:452
  61.7 37.0 %place.1 = (f32[9,2,64,128]{3,2,1,0:T(8,128)}, f32[9,2,64,128]{3,2,1,0:T(8,128)}) custom-call(f32[9,2,64,128]{3,2,1,0:T(8,128)} %get-tuple-element.4.smoothed, f32[9,2,64,128]{3,2,1,0:T(8,128)} %get-tuple-element.5.residual), custom_call_target="tpu_custom_call" | custom-call | tf_op jit(solution)/shard_map/place/pallas_call | solution.py:480

commit v7 on v5

--- a/solution.py
+++ b/solution.py
@@ -418,6 +418,23 @@
     for i in range(planes):
         for copy in results(i):
             copy.wait()
+
+
+def place(smoothed, residual, smoothed_out, residual_out, held, sem):
+    triples = [
+        (ref.at[j], held.at[n, j], out.at[j], sem.at[n, j])
+        for j in range(smoothed.shape[0])
+        for n, (ref, out) in enumerate(((smoothed, smoothed_out), (residual, residual_out)))
+    ]
+    inward = [pltpu.make_async_copy(ref, kept, which.at[0]) for ref, kept, _, which in triples]
+    outward = [pltpu.make_async_copy(kept, out, which.at[1]) for _, kept, out, which in triples]
+    for copy in inward:
+        copy.start()
+    for arriving, leaving in zip(inward, outward):
+        arriving.wait()
+        leaving.start()
+    for copy in outward:
+        copy.wait()
 
 
 def body(count, start_field, source, mean_field, kl_fields, triples, coef):
@@ -462,7 +479,15 @@
         ),
         name="sweeps",
     )(triples.T, coef[None], start_field, source, mean_field, kl_fields)
-    return smoothed, residual
+    return pl.pallas_call(
+        place,
+        out_shape=(whole, whole),
+        in_specs=[anywhere, anywhere],
+        out_specs=(anywhere, anywhere),
+        scratch_shapes=[pltpu.VMEM((2, *start_field.shape), f32), dma((2, local, 2))],
+        compiler_params=pltpu.CompilerParams(vmem_limit_bytes=62 * 1024 * 1024),
+        name="place",
+    )(smoothed, residual)
 
 
 def solution(mesh):

time: 63.8 us -> 63.3 us (level)
  local copies, waits for them, and re-layouts: 2.81 us -> 0 us
  Pallas kernels: 60.2 us -> 62.5 us
    unnamed x4 -> x0, local copies, waits for them, and re-layouts: 2.81 us -> none
    pallas_call x0 -> x1, Pallas kernels: none -> 2.23 us  [body(): pl.pallas_call(place, out_shape=(whole, whole), in_specs=[anywhere, anywh...]
where the time goes in v7:
time: 63.3 us; the launch traced here: 63.1 us
  Pallas kernels  62.5 us (99%)
  between operations  0.64 us (1%)
    pallas_call x1, Pallas kernels, body(): pl.pallas_call(functools.partial(kernel, groups, count), out_shape=(whole...  60.2 us
    pallas_call x1, Pallas kernels, body(): pl.pallas_call(place, out_shape=(whole, whole), in_specs=[anywhere, anywh...  2.23 us

profile of v7, /device:TPU:0, one launch (start us, length us, event | category | flops | bytes accessed | tf_op | source)
XLA Modules:
  0.0 63.1 jit_solution(5846877089234427897)
XLA Ops:
  0.6 60.2 %sweeps.1 = (f32[9,2,64,128]{3,2,1,0:T(8,128)}, f32[9,2,64,128]{3,2,1,0:T(8,128)}) custom-call(s32[3,156]{1,0:T(4,128)} %bitcast.2, f32[1,156]{1,0:T(1,128)} %bitcast.3, f32[9,2,64,128]{3,2,1,0:T(8,128)} %start.1, f32[9,2,64,128]{3,2,1,0:T(8,128)} %source.1, f32[2,64,128]{2,1,0:T(8,128)} %mean.1, f32[4,2,64,128]{3,2,1,0:T(8,128)} %kl.1), custom_call_target="tpu_custom_call" | custom-call | tf_op jit(solution)/shard_map/sweeps/pallas_call | solution.py:454
  60.9 2.2 %place.1 = (f32[9,2,64,128]{3,2,1,0:T(8,128)}, f32[9,2,64,128]{3,2,1,0:T(8,128)}) custom-call(f32[9,2,64,128]{3,2,1,0:T(8,128)} %get-tuple-element.4.smoothed, f32[9,2,64,128]{3,2,1,0:T(8,128)} %get-tuple-element.5.residual), custom_call_target="tpu_custom_call" | custom-call | tf_op jit(solution)/shard_map/place/pallas_call | solution.py:482

commit v8 on v7

--- a/solution.py
+++ b/solution.py
@@ -360,7 +360,7 @@
             sweep(k, i, out, 0, 2, quads - 1)
             done(i)
 
-    sweep_all(0, out_first, lambda i: None)
+    sweep_all(0, out_first, lambda i: trade_start(2, i) if i == 0 else None)
 
     def update(z, y):
         inverse = spread_weights(z, y)[(FACES + 1) * nfields:(FACES + 1) * nfields + 1]
@@ -371,7 +371,10 @@
     for i in range(planes):
         trade_wait_recv(1, i)
         fill_plane(1, i, update)
-        trade_start(2, i, after=(1, i))
+        if i == 0:
+            trade_wait_send(1, 0)
+        else:
+            trade_start(2, i, after=(1, i))
     sweep_all(1, out_second, lambda i: trade_start(3, i))
 
     for copy in fields_here:

time: 63.3 us -> 62.9 us (level)
  no operation moved by 1% of the time
where the time goes in v8:
time: 62.9 us; the launch traced here: 62.8 us
  Pallas kernels  62.1 us (99%)
  between operations  0.64 us (1%)
    pallas_call x1, Pallas kernels, body(): pl.pallas_call(functools.partial(kernel, groups, count), out_shape=(whole...  59.9 us
    pallas_call x1, Pallas kernels, body(): pl.pallas_call(place, out_shape=(whole, whole), in_specs=[anywhere, anywh...  2.23 us

profile of v8, /device:TPU:0, one launch (start us, length us, event | category | flops | bytes accessed | tf_op | source)
XLA Modules:
  0.0 62.8 jit_solution(753421492542601686)
XLA Ops:
  0.6 59.9 %sweeps.1 = (f32[9,2,64,128]{3,2,1,0:T(8,128)}, f32[9,2,64,128]{3,2,1,0:T(8,128)}) custom-call(s32[3,156]{1,0:T(4,128)} %bitcast.2, f32[1,156]{1,0:T(1,128)} %bitcast.3, f32[9,2,64,128]{3,2,1,0:T(8,128)} %start.1, f32[9,2,64,128]{3,2,1,0:T(8,128)} %source.1, f32[2,64,128]{2,1,0:T(8,128)} %mean.1, f32[4,2,64,128]{3,2,1,0:T(8,128)} %kl.1), custom_call_target="tpu_custom_call" | custom-call | tf_op jit(solution)/shard_map/sweeps/pallas_call | solution.py:457
  60.5 2.2 %place.1 = (f32[9,2,64,128]{3,2,1,0:T(8,128)}, f32[9,2,64,128]{3,2,1,0:T(8,128)}) custom-call(f32[9,2,64,128]{3,2,1,0:T(8,128)} %get-tuple-element.4.smoothed, f32[9,2,64,128]{3,2,1,0:T(8,128)} %get-tuple-element.5.residual), custom_call_target="tpu_custom_call" | custom-call | tf_op jit(solution)/shard_map/place/pallas_call | solution.py:485

commit v9 on v8

--- a/solution.py
+++ b/solution.py
@@ -262,7 +262,7 @@
         def inner(y, carry):
             one_row(z, y)
             return carry
-        lax.fori_loop(1, rows - 1, inner, 0)
+        lax.fori_loop(1, rows - 1, inner, 0, unroll=7)
         if i == 0:
             plane_start(k, far)
         if i == planes - 1:

time: 62.9 us -> 63.2 us (level)
  no operation moved by 1% of the time
where the time goes in v9:
time: 63.2 us; the launch traced here: 63 us
  Pallas kernels  62.4 us (99%)
  between operations  0.64 us (1%)
    pallas_call x1, Pallas kernels, body(): pl.pallas_call(functools.partial(kernel, groups, count), out_shape=(whole...  60.1 us
    pallas_call x1, Pallas kernels, body(): pl.pallas_call(place, out_shape=(whole, whole), in_specs=[anywhere, anywh...  2.23 us

profile of v9, /device:TPU:0, one launch (start us, length us, event | category | flops | bytes accessed | tf_op | source)
XLA Modules:
  0.0 63.0 jit_solution(1384033813151754485)
XLA Ops:
  0.6 60.1 %sweeps.1 = (f32[9,2,64,128]{3,2,1,0:T(8,128)}, f32[9,2,64,128]{3,2,1,0:T(8,128)}) custom-call(s32[3,156]{1,0:T(4,128)} %bitcast.2, f32[1,156]{1,0:T(1,128)} %bitcast.3, f32[9,2,64,128]{3,2,1,0:T(8,128)} %start.1, f32[9,2,64,128]{3,2,1,0:T(8,128)} %source.1, f32[2,64,128]{2,1,0:T(8,128)} %mean.1, f32[4,2,64,128]{3,2,1,0:T(8,128)} %kl.1), custom_call_target="tpu_custom_call" | custom-call | tf_op jit(solution)/shard_map/sweeps/pallas_call | solution.py:457
  60.8 2.2 %place.1 = (f32[9,2,64,128]{3,2,1,0:T(8,128)}, f32[9,2,64,128]{3,2,1,0:T(8,128)}) custom-call(f32[9,2,64,128]{3,2,1,0:T(8,128)} %get-tuple-element.4.smoothed, f32[9,2,64,128]{3,2,1,0:T(8,128)} %get-tuple-element.5.residual), custom_call_target="tpu_custom_call" | custom-call | tf_op jit(solution)/shard_map/place/pallas_call | solution.py:485
